TPU v7x, 32 devices: a whole 2x2x4 slice. The times are simulated.
32 devices in a mesh: member: 2 (over x), lat: 16 (over z, y, core).
Axes of the slice: x: 2, y: 2, z: 4, core: 2. Of those that a mesh axis runs over, the one named last changes fastest.
Arguments:
- atmosphere: float32 [2, 4, 8, 96, 1536], P(None, 'member', None, 'lat'), may hold values from -4 to 4
- ocean_state: float32 [2, 96, 1536], P(None, 'lat', 'member'), may hold values from -4 to 4
- viscosity: float32 [96, 1536], P('lat', 'member'), may hold values from 0.02 to 0.2
- sea_mask: int32 [96, 1536], P('lat'), may hold values 0 or 1
- parameter_index: int32 [4], P('member'), may hold values from 0 to 31
- parameter_table: float32 [32, 3], replicated, may hold values from 0.1 to 0.3
- level_mix: float32 [8, 8], replicated, may hold values from -0.5 to 0.5
Outputs:
- atmos_out: float32 [2, 4, 8, 96, 1536], P(None, 'member', None, 'lat')
- ocean_out: float32 [2, 96, 1536], P(None, 'lat', 'member')
All inputs are finite; a program needn't handle non-finite values. No bound on the sum of `sea_mask` on one device may be relied on, other than what follows from the above.
Results may differ from a plain program's by a relative error of at most 0.00011.
Values sent between devices are 32-bit elements; how exact they have to be, the bound alone decides.
No kernel may reach another device: no remote copies, remote signals or barrier semaphores. Data moves between devices by JAX's collectives and lax.ppermute only.
A program may use at most 64 MiB of HBM per device.

v0:
```python
import jax
import jax.numpy as jnp
from jax import lax
from jax.sharding import PartitionSpec as P

ASTEPS = 3
OSTEPS = 2
COUPLE = 2


ADVECTION = 0.1
OCEAN_GAIN = 0.5
OCEAN_DIFFUSION = 0.15


def with_halo(block, sides, width, periodic):
    for axis, dim in sides:
        count = lax.axis_size(axis)
        forward = [(i, i + 1) for i in range(count - 1)]
        if periodic:
            forward.append((count - 1, 0))
        backward = [(target, source) for source, target in forward]
        low = lax.ppermute(
            lax.slice_in_dim(block, block.shape[dim] - width, None, axis=dim), axis, forward
        )
        high = lax.ppermute(lax.slice_in_dim(block, 0, width, axis=dim), axis, backward)
        block = jnp.concatenate([low, block, high], axis=dim)
    return block


def lookup(parameter_index, parameter_table):
    onehot = (
        parameter_index[:, None] == jnp.arange(parameter_table.shape[0], dtype=jnp.int32)[None, :]
    ).astype(jnp.float32)
    picked = jnp.dot(
        onehot, parameter_table, precision=lax.Precision.HIGHEST, preferred_element_type=jnp.float32
    )
    return (0.6 * picked[:, 0], 2.0 * jnp.transpose(picked[:, 1:3]))


def atmos_step(padded_rows, surface, diffusivity, exchange, level_mix):
    centre = padded_rows[:, :, :, 1:-1, :]
    northern = padded_rows[:, :, :, 2:, :]
    southern = padded_rows[:, :, :, :-2, :]
    eastern = jnp.roll(centre, -1, axis=4)
    western = jnp.roll(centre, 1, axis=4)
    laplace = eastern + western + northern + southern - 4.0 * centre
    zonal_wind = centre[1]
    advected = (
        centre
        - ADVECTION * zonal_wind[None] * (eastern - western) * 0.5
        + diffusivity[None, :, None, None, None] * laplace
    )
    mixed_state = advected + jnp.einsum(
        "kl,fmlrn->fmkrn", level_mix, advected, precision=lax.Precision.HIGHEST
    )
    bottom = mixed_state[:, :, 0] + exchange[:, :, None, None] * (
        surface[:, None] - mixed_state[:, :, 0]
    )
    return mixed_state.at[:, :, 0].set(bottom)


def atmos_window(atmos_state, surface, diffusivity, exchange, level_mix):
    local_rows = atmos_state.shape[3]
    extended = with_halo(atmos_state, (("lat", 3),), ASTEPS, False)
    surface_rows = with_halo(surface, (("lat", 1),), ASTEPS, False)
    total_rows = local_rows * lax.axis_size("lat")
    first_row = lax.axis_index("lat") * local_rows - ASTEPS
    for substep in range(ASTEPS):
        row_count = extended.shape[3] - 2
        centre_surface = surface_rows[:, substep + 1 : substep + 1 + row_count]
        extended = atmos_step(extended, centre_surface, diffusivity, exchange, level_mix)
        global_row = first_row + substep + 1 + jnp.arange(row_count, dtype=jnp.int32)
        inside = ((global_row >= 0) & (global_row < total_rows)).astype(jnp.float32)
        extended = extended * inside[:, None]
    return extended


def ocean_step(ocean, forcing, ocean_rate, ocean_mask):
    padded_ocean = with_halo(ocean, (("lat", 1),), 1, False)
    columns = with_halo(ocean, (("member", 2),), 1, True)
    eastern = columns[:, :, 2:]
    western = columns[:, :, :-2]
    laplace = padded_ocean[:, 2:] + padded_ocean[:, :-2] + eastern + western - 4.0 * ocean
    return ocean + ocean_mask[None] * (OCEAN_GAIN * forcing + ocean_rate * laplace)


def body(atmosphere, ocean_state, viscosity, sea_mask, parameter_index, parameter_table, level_mix):
    local_members = atmosphere.shape[1]
    tile_width = ocean_state.shape[2]
    members = local_members * lax.axis_size("member")
    diffusivity, exchange = lookup(parameter_index, parameter_table)
    full_mask = sea_mask.astype(jnp.float32)
    tile_start = lax.axis_index("member") * tile_width
    ocean = ocean_state
    ocean_mask = lax.dynamic_slice_in_dim(full_mask, tile_start, tile_width, 1)
    ocean_rate = jnp.stack([jnp.full_like(viscosity, OCEAN_DIFFUSION), viscosity])
    atmos_state = atmosphere
    for coupling in range(COUPLE):
        surface = lax.all_gather(ocean, "member", axis=2, tiled=True)
        atmos_state = atmos_window(atmos_state, surface, diffusivity, exchange, level_mix)
        flux_terms = jnp.sum(
            exchange[:, :, None, None] * (atmos_state[:, :, 0] - surface[:, None]), axis=1
        )
        forcing = lax.psum_scatter(flux_terms, "member", scatter_dimension=2, tiled=True) / members
        for substep in range(OSTEPS):
            ocean = ocean_step(ocean, forcing, ocean_rate, ocean_mask)
    return (atmos_state, ocean)


def solution(mesh):
    return jax.shard_map(
        body,
        mesh=mesh,
        in_specs=(
            P(None, "member", None, "lat", None),
            P(None, "lat", "member"),
            P("lat", "member"),
            P("lat", None),
            P("member"),
            P(),
            P(),
        ),
        out_specs=(P(None, "member", None, "lat", None), P(None, "lat", "member")),
        check_vma=False,
    )
```

profile of v0, /device:TPU:8, one launch (start us, length us, event | category | flops | bytes accessed | tf_op | source)
XLA Modules:
  0.0 152.6 jit_solution(7470134454339684033)
XLA Ops:
  7.3 2.3 %fusion.178 = (f32[2,2,8,3,1536]{4,2,3,1,0:T(8,128)}, f32[2,2,8,3,1536]{4,2,3,1,0:T(8,128)}) fusion(f32[2,2,8,6,1536]{4,2,3,1,0:T(8,128)} %param.19), kind=kLoop, calls=%fused_computation.256 | loop fusion | bytes 2359296 | tf_op jit(solution)/shard_map/slice | solution.py:26
  11.5 4.7 %collective-permute-start.1 = (f32[2,2,8,3,1536]{4,2,3,1,0:T(8,128)}, f32[2,2,8,3,1536]{4,2,3,1,0:T(8,128)S(1)}, u32[]{:S(2)}, u32[]{:S(2)}) collective-permute-start(f32[2,2,8,3,1536]{4,2,3,1,0:T(8,128)} %get-tuple-element.104), channel_id=1, source_target_pairs={{1,0},{2,1},{3,2},{4,3},{5,4},{6,5},{7,6},{8,7},{9,8},{10,9},{11,1... | collective-permute-start | bytes 1769480 | tf_op jit(solution)/shard_map/ppermute | solution.py:26
  16.2 4.6 %all_gather.6 = f32[2,6,1536]{2,0,1:T(2,128)S(1)} all-gather(f32[2,6,768]{2,0,1:T(2,128)S(1)} %copy-done.8), channel_id=1, replica_groups=mesh['member'=2,'lat'=16] {'member'}, dimensions={2}, use_global_device_ids=true | all-gather | bytes 110592 | tf_op jit(solution)/shard_map/all_gather | solution.py:100
  22.8 4.5 %collective-permute-start.3 = (f32[2,3,1536]{2,0,1:T(2,128)S(1)}, f32[2,3,1536]{2,0,1:T(2,128)S(1)}, u32[]{:S(2)}, u32[]{:S(2)}) collective-permute-start(f32[2,3,1536]{2,0,1:T(2,128)S(1)} %get-tuple-element.108), channel_id=1, source_target_pairs={{1,0},{2,1},{3,2},{4,3},{5,4},{6,5},{7,6},{8,7},{9,8},{10,9},{11,1... | collective-permute-start | bytes 110600 | tf_op jit(solution)/shard_map/ppermute | solution.py:26
  32.2 4.5 %collective-permute-start.6 = (f32[2,1,768]{2,1,0:T(1,128)S(1)}, f32[2,1,768]{2,1,0:T(1,128)S(1)}, u32[]{:S(2)}, u32[]{:S(2)}) collective-permute-start(f32[2,1,768]{2,1,0:T(1,128)S(1)} %copy.97), channel_id=1, source_target_pairs={{1,0},{2,1},{3,2},{4,3},{5,4},{6,5},{7,6},{8,7},{9,8},{10,9},{11,1... | collective-permute-start | bytes 18440 | tf_op jit(solution)/shard_map/ppermute | solution.py:26
  37.9 4.2 %fusion.1 = f32[2,2,8,10,1536]{4,2,3,1,0:T(8,128)S(1)} fusion(f32[2,2,8,12,1536]{4,2,3,1,0:T(8,128)S(1)} %constant_dynamic-update-slice_fusion, f32[2,2,8,10,1535]{4,2,3,1,0:T(8,128)S(1)} %get-tuple-element.83, f32[2,2,8,10,1]{4,2,3,1,0:T(8,128)S(1)} %get-tuple-element.85, f32[2,2,8,10,1]{4,2,3,1,0:T(8,128)S(1)} %get-tuple-element.84, ...), kind=kOutput, calls=%fused_computation.3 | convolution fusion | flops 60456960 | bytes 24253440 | tf_op jit(solution)/shard_map/kl,fmlrn->fmkrn/dot_general | solution.py:54
  42.5 2.5 %scatter.20 = f32[2,2,8,10,1536]{4,2,3,1,0:T(8,128)S(1)} dynamic-update-slice(f32[2,2,8,10,1536]{4,2,3,1,0:T(8,128)S(1)} %fusion.1, f32[2,2,1,10,1536]{4,2,3,1,0:T(1,128)S(1)} %multiply_add_fusion.1, s32[]{:T(128)} %constant.175.clone.1, s32[]{:T(128)} %constant.175.clone.1, s32[]{:T(128)} %constant.175.clone.1, s32[]{:T(128)} %constant.175.clone.1, s32[]{:T(128)} %constant.175.clone.1) | dynamic-update-slice | bytes 491524 | tf_op jit(solution)/shard_map/scatter | solution.py:60
  46.1 3.4 %fusion.3 = f32[2,2,8,8,1536]{4,2,3,1,0:T(8,128)S(1)} fusion(f32[2,2,8,10,1536]{4,2,3,1,0:T(8,128)S(1)} %broadcast_multiply_fusion.1, f32[2,2,8,8,1535]{4,2,3,1,0:T(8,128)S(1)} %get-tuple-element.91, f32[2,2,8,8,1]{4,2,3,1,0:T(8,128)S(1)} %get-tuple-element.93, f32[2,2,8,8,1]{4,2,3,1,0:T(8,128)S(1)} %get-tuple-element.92, ...), kind=kOutput, calls=%fused_computation.7 | convolution fusion | flops 48365568 | bytes 19403776 | tf_op jit(solution)/shard_map/kl,fmlrn->fmkrn/dot_general | solution.py:54
  49.9 2.2 %scatter.21 = f32[2,2,8,8,1536]{4,2,3,1,0:T(8,128)S(1)} dynamic-update-slice(f32[2,2,8,8,1536]{4,2,3,1,0:T(8,128)S(1)} %fusion.3, f32[2,2,1,8,1536]{4,2,3,1,0:T(1,128)S(1)} %multiply_add_fusion.3, s32[]{:T(128)} %constant.175.clone.1, s32[]{:T(128)} %constant.175.clone.1, s32[]{:T(128)} %constant.175.clone.1, s32[]{:T(128)} %constant.175.clone.1, s32[]{:T(128)} %constant.175.clone.1) | dynamic-update-slice | bytes 393220 | tf_op jit(solution)/shard_map/scatter | solution.py:60
  52.9 2.5 %fusion.5 = f32[2,2,8,6,1536]{4,2,3,1,0:T(8,128)S(1)} fusion(f32[2,2,8,8,1536]{4,2,3,1,0:T(8,128)S(1)} %broadcast_multiply_fusion.3, f32[2,2,8,6,1535]{4,2,3,1,0:T(8,128)S(1)} %get-tuple-element.99, f32[2,2,8,6,1]{4,2,3,1,0:T(8,128)S(1)} %get-tuple-element.101, f32[2,2,8,6,1]{4,2,3,1,0:T(8,128)S(1)} %get-tuple-element.100, ...), kind=kOutput, calls=%fused_computation.11 | convolution fusion | flops 36274176 | bytes 14554112 | tf_op jit(solution)/shard_map/kl,fmlrn->fmkrn/dot_general | solution.py:54
  60.8 2.4 %collective-permute-start.4 = (f32[2,2,8,3,1536]{4,2,3,1,0:T(8,128)S(1)}, f32[2,2,8,3,1536]{4,2,3,1,0:T(8,128)S(1)}, u32[]{:S(2)}, u32[]{:S(2)}) collective-permute-start(f32[2,2,8,3,1536]{4,2,3,1,0:T(8,128)S(1)} %get-tuple-element.102), channel_id=1, source_target_pairs={{0,1},{1,2},{2,3},{3,4},{4,5},{5,6},{6,7},{7,8},{8,9},{9,10},{10,1... | collective-permute-start | bytes 1769480 | tf_op jit(solution)/shard_map/ppermute | solution.py:23
  63.3 5.0 %reduce-scatter.3.cloned.1.call-done = f32[2,6,768]{2,1,0:T(8,128)} async-done(((f32[2,6,1536]{2,1,0:T(8,128)}), f32[2,6,768]{2,1,0:T(8,128)}) %reduce-scatter.3.cloned.1.call-update) | async-done | bytes 36880 | tf_op jit(solution)/shard_map/reduce_scatter | solution.py:105
  71.2 4.5 %collective-permute-start.10 = (f32[2,1,768]{2,1,0:T(1,128)S(1)}, f32[2,1,768]{2,1,0:T(1,128)S(1)}, u32[]{:S(2)}, u32[]{:S(2)}) collective-permute-start(f32[2,1,768]{2,1,0:T(1,128)S(1)} %get-tuple-element.118), channel_id=1, source_target_pairs={{1,0},{2,1},{3,2},{4,3},{5,4},{6,5},{7,6},{8,7},{9,8},{10,9},{11,1... | collective-permute-start | bytes 18440 | tf_op jit(solution)/shard_map/ppermute | solution.py:26
  76.3 3.1 %collective-permute-done.13 = f32[2,6,1]{2,1,0:T(8,128)S(1)} collective-permute-done((f32[2,6,1]{2,1,0:T(8,128)S(1)}, f32[2,6,1]{2,1,0:T(8,128)S(1)}, u32[]{:S(2)}, u32[]{:S(2)}) %collective-permute-start.13) | collective-permute-done | bytes 80 | tf_op jit(solution)/shard_map/ppermute | solution.py:23
  80.0 3.1 %collective-permute-done.12 = f32[2,6,1]{2,1,0:T(8,128)S(1)} collective-permute-done((f32[2,6,1]{2,1,0:T(8,128)S(1)}, f32[2,6,1]{2,1,0:T(8,128)S(1)}, u32[]{:S(2)}, u32[]{:S(2)}) %collective-permute-start.12) | collective-permute-done | bytes 80 | tf_op jit(solution)/shard_map/ppermute | solution.py:26
  84.0 4.8 %all_gather.7 = f32[2,6,1536]{2,1,0:T(8,128)S(1)} all-gather(f32[2,6,768]{2,1,0:T(8,128)S(1)} %fusion.115), channel_id=1, replica_groups=mesh['member'=2,'lat'=16] {'member'}, dimensions={2}, use_global_device_ids=true | all-gather | bytes 110592 | tf_op jit(solution)/shard_map/all_gather | solution.py:100
  90.7 2.4 %collective-permute-start.14 = (f32[2,3,1536]{2,1,0:T(4,128)S(1)}, f32[2,3,1536]{2,1,0:T(4,128)S(1)}, u32[]{:S(2)}, u32[]{:S(2)}) collective-permute-start(f32[2,3,1536]{2,1,0:T(4,128)S(1)} %get-tuple-element.106), channel_id=1, source_target_pairs={{0,1},{1,2},{2,3},{3,4},{4,5},{5,6},{6,7},{7,8},{8,9},{9,10},{10,1... | collective-permute-start | bytes 110600 | tf_op jit(solution)/shard_map/ppermute | solution.py:23
  95.3 4.4 %collective-permute-start.16 = (f32[2,1,768]{2,1,0:T(1,128)S(1)}, f32[2,1,768]{2,1,0:T(1,128)S(1)}, u32[]{:S(2)}, u32[]{:S(2)}) collective-permute-start(f32[2,1,768]{2,1,0:T(1,128)S(1)} %get-tuple-element.114), channel_id=1, source_target_pairs={{1,0},{2,1},{3,2},{4,3},{5,4},{6,5},{7,6},{8,7},{9,8},{10,9},{11,1... | collective-permute-start | bytes 18440 | tf_op jit(solution)/shard_map/ppermute | solution.py:26
  102.8 4.6 %fusion = f32[2,2,8,10,1536]{4,2,3,1,0:T(8,128)S(1)} fusion(f32[2,2,8,12,1536]{4,2,3,1,0:T(8,128)S(1)} %pad_maximum_fusion, f32[2,2,8,3,1536]{4,2,3,1,0:T(8,128)S(1)} %copy-done.4, f32[2,2,8,6,1536]{4,2,3,1,0:T(8,128)S(1)} %broadcast_multiply_fusion.5, f32[2,2,8,3,1536]{4,2,3,1,0:T(8,128)S(1)} %copy-done.6, ...), kind=kOutput, calls=%fused_computation.1 | convolution fusion | flops 64389120 | bytes 28316672 | tf_op jit(solution)/shard_map/kl,fmlrn->fmkrn/dot_general | solution.py:54
  107.8 2.5 %scatter.25 = f32[2,2,8,10,1536]{4,2,3,1,0:T(8,128)S(1)} dynamic-update-slice(f32[2,2,8,10,1536]{4,2,3,1,0:T(8,128)S(1)} %fusion, f32[2,2,1,10,1536]{4,2,3,1,0:T(1,128)S(1)} %multiply_add_fusion, s32[]{:T(128)} %constant.175.clone.1, s32[]{:T(128)} %constant.175.clone.1, s32[]{:T(128)} %constant.175.clone.1, s32[]{:T(128)} %constant.175.clone.1, s32[]{:T(128)} %constant.175.clone.1) | dynamic-update-slice | bytes 491524 | tf_op jit(solution)/shard_map/scatter | solution.py:60
  111.4 3.4 %fusion.2 = f32[2,2,8,8,1536]{4,2,3,1,0:T(8,128)S(1)} fusion(f32[2,2,8,10,1536]{4,2,3,1,0:T(8,128)S(1)} %broadcast_multiply_fusion, f32[2,2,8,8,1535]{4,2,3,1,0:T(8,128)S(1)} %get-tuple-element.87, f32[2,2,8,8,1]{4,2,3,1,0:T(8,128)S(1)} %get-tuple-element.89, f32[2,2,8,8,1]{4,2,3,1,0:T(8,128)S(1)} %get-tuple-element.88, ...), kind=kOutput, calls=%fused_computation.5 | convolution fusion | flops 48365568 | bytes 19403776 | tf_op jit(solution)/shard_map/kl,fmlrn->fmkrn/dot_general | solution.py:54
  118.2 2.5 %fusion.4 = f32[2,2,8,6,1536]{4,2,3,1,0:T(8,128)S(1)} fusion(f32[2,2,8,8,1536]{4,2,3,1,0:T(8,128)S(1)} %broadcast_multiply_fusion.2, f32[2,2,8,6,1535]{4,2,3,1,0:T(8,128)S(1)} %get-tuple-element.95, f32[2,2,8,6,1]{4,2,3,1,0:T(8,128)S(1)} %get-tuple-element.97, f32[2,2,8,6,1]{4,2,3,1,0:T(8,128)S(1)} %get-tuple-element.96, ...), kind=kOutput, calls=%fused_computation.9 | convolution fusion | flops 36274176 | bytes 14554112 | tf_op jit(solution)/shard_map/kl,fmlrn->fmkrn/dot_general | solution.py:54
  127.5 5.0 %reduce-scatter.5.cloned.1.call-done = f32[2,6,768]{2,1,0:T(8,128)} async-done(((f32[2,6,1536]{2,1,0:T(8,128)}), f32[2,6,768]{2,1,0:T(8,128)}) %reduce-scatter.5.cloned.1.call-update) | async-done | bytes 36880 | tf_op jit(solution)/shard_map/reduce_scatter | solution.py:105
  135.4 4.5 %collective-permute-start.20 = (f32[2,1,768]{2,1,0:T(1,128)S(1)}, f32[2,1,768]{2,1,0:T(1,128)S(1)}, u32[]{:S(2)}, u32[]{:S(2)}) collective-permute-start(f32[2,1,768]{2,1,0:T(1,128)S(1)} %get-tuple-element.110), channel_id=1, source_target_pairs={{1,0},{2,1},{3,2},{4,3},{5,4},{6,5},{7,6},{8,7},{9,8},{10,9},{11,1... | collective-permute-start | bytes 18440 | tf_op jit(solution)/shard_map/ppermute | solution.py:26
  (144 shorter events, 49.9 us)
Async XLA Ops:
  7.2 61.1 %reduce-scatter.3.cloned.1.call-start = ((), (), s32[]{:S(2)}) async-start(), calls=%async_computation.2 | async-start | bytes 147456 | tf_op jit(solution)/shard_map/reduce_scatter | solution.py:105
  9.6 22.6 %collective-permute-start = (f32[2,2,8,3,1536]{4,2,3,1,0:T(8,128)}, f32[2,2,8,3,1536]{4,2,3,1,0:T(8,128)S(1)}, u32[]{:S(2)}, u32[]{:S(2)}) collective-permute-start(f32[2,2,8,3,1536]{4,2,3,1,0:T(8,128)} %get-tuple-element.105), channel_id=1, source_target_pairs={{0,1},{1,2},{2,3},{3,4},{4,5},{5,6},{6,7},{7,8},{8,9},{9,10},{10,1... | collective-permute-start | bytes 1769480 | tf_op jit(solution)/shard_map/ppermute | solution.py:23
  11.5 25.4 %collective-permute-start.1 = (f32[2,2,8,3,1536]{4,2,3,1,0:T(8,128)}, f32[2,2,8,3,1536]{4,2,3,1,0:T(8,128)S(1)}, u32[]{:S(2)}, u32[]{:S(2)}) collective-permute-start(f32[2,2,8,3,1536]{4,2,3,1,0:T(8,128)} %get-tuple-element.104), channel_id=1, source_target_pairs={{1,0},{2,1},{3,2},{4,3},{5,4},{6,5},{7,6},{8,7},{9,8},{10,9},{11,1... | collective-permute-start | bytes 1769480 | tf_op jit(solution)/shard_map/ppermute | solution.py:26
  20.9 8.7 %collective-permute-start.2 = (f32[2,3,1536]{2,0,1:T(2,128)S(1)}, f32[2,3,1536]{2,0,1:T(2,128)S(1)}, u32[]{:S(2)}, u32[]{:S(2)}) collective-permute-start(f32[2,3,1536]{2,0,1:T(2,128)S(1)} %get-tuple-element.109), channel_id=1, source_target_pairs={{0,1},{1,2},{2,3},{3,4},{4,5},{5,6},{6,7},{7,8},{8,9},{9,10},{10,1... | collective-permute-start | bytes 110600 | tf_op jit(solution)/shard_map/ppermute | solution.py:23
  22.8 7.4 %collective-permute-start.3 = (f32[2,3,1536]{2,0,1:T(2,128)S(1)}, f32[2,3,1536]{2,0,1:T(2,128)S(1)}, u32[]{:S(2)}, u32[]{:S(2)}) collective-permute-start(f32[2,3,1536]{2,0,1:T(2,128)S(1)} %get-tuple-element.108), channel_id=1, source_target_pairs={{1,0},{2,1},{3,2},{4,3},{5,4},{6,5},{7,6},{8,7},{9,8},{10,9},{11,1... | collective-permute-start | bytes 110600 | tf_op jit(solution)/shard_map/ppermute | solution.py:26
  27.4 33.4 %collective-permute-start.9 = (f32[2,6,1]{2,1,0:T(8,128)S(1)}, f32[2,6,1]{2,1,0:T(8,128)S(1)}, u32[]{:S(2)}, u32[]{:S(2)}) collective-permute-start(f32[2,6,1]{2,1,0:T(8,128)S(1)} %get-tuple-element.123), channel_id=1, source_target_pairs={{0,16},{16,0},{1,17},{17,1},{2,18},{18,2},{3,19},{19,3},{4,20},{20... | collective-permute-start | bytes 152 | tf_op jit(solution)/shard_map/ppermute | solution.py:23
  29.5 33.7 %collective-permute-start.8 = (f32[2,6,1]{2,1,0:T(8,128)S(1)}, f32[2,6,1]{2,1,0:T(8,128)S(1)}, u32[]{:S(2)}, u32[]{:S(2)}) collective-permute-start(f32[2,6,1]{2,1,0:T(8,128)S(1)} %get-tuple-element.122), channel_id=1, source_target_pairs={{16,0},{0,16},{17,1},{1,17},{18,2},{2,18},{19,3},{3,19},{20,4},{4,... | collective-permute-start | bytes 152 | tf_op jit(solution)/shard_map/ppermute | solution.py:26
  30.2 33.1 %collective-permute-start.7 = (f32[2,1,768]{2,1,0:T(1,128)S(1)}, f32[2,1,768]{2,1,0:T(1,128)S(1)}, u32[]{:S(2)}, u32[]{:S(2)}) collective-permute-start(f32[2,1,768]{2,1,0:T(1,128)S(1)} %copy.99), channel_id=1, source_target_pairs={{0,1},{1,2},{2,3},{3,4},{4,5},{5,6},{6,7},{7,8},{8,9},{9,10},{10,1... | collective-permute-start | bytes 18440 | tf_op jit(solution)/shard_map/ppermute | solution.py:23
  32.2 31.1 %collective-permute-start.6 = (f32[2,1,768]{2,1,0:T(1,128)S(1)}, f32[2,1,768]{2,1,0:T(1,128)S(1)}, u32[]{:S(2)}, u32[]{:S(2)}) collective-permute-start(f32[2,1,768]{2,1,0:T(1,128)S(1)} %copy.97), channel_id=1, source_target_pairs={{1,0},{2,1},{3,2},{4,3},{5,4},{6,5},{7,6},{8,7},{9,8},{10,9},{11,1... | collective-permute-start | bytes 18440 | tf_op jit(solution)/shard_map/ppermute | solution.py:26
  58.0 74.5 %reduce-scatter.5.cloned.1.call-start = ((), (), s32[]{:S(2)}) async-start(), calls=%async_computation.3 | async-start | bytes 147456 | tf_op jit(solution)/shard_map/reduce_scatter | solution.py:105
  58.9 40.9 %collective-permute-start.5 = (f32[2,2,8,3,1536]{4,2,3,1,0:T(8,128)}, f32[2,2,8,3,1536]{4,2,3,1,0:T(8,128)S(1)}, u32[]{:S(2)}, u32[]{:S(2)}) collective-permute-start(f32[2,2,8,3,1536]{4,2,3,1,0:T(8,128)} %get-tuple-element.103), channel_id=1, source_target_pairs={{1,0},{2,1},{3,2},{4,3},{5,4},{6,5},{7,6},{8,7},{9,8},{10,9},{11,1... | collective-permute-start | bytes 1769480 | tf_op jit(solution)/shard_map/ppermute | solution.py:26
  60.8 39.0 %collective-permute-start.4 = (f32[2,2,8,3,1536]{4,2,3,1,0:T(8,128)S(1)}, f32[2,2,8,3,1536]{4,2,3,1,0:T(8,128)S(1)}, u32[]{:S(2)}, u32[]{:S(2)}) collective-permute-start(f32[2,2,8,3,1536]{4,2,3,1,0:T(8,128)S(1)} %get-tuple-element.102), channel_id=1, source_target_pairs={{0,1},{1,2},{2,3},{3,4},{4,5},{5,6},{6,7},{7,8},{8,9},{9,10},{10,1... | collective-permute-start | bytes 1769480 | tf_op jit(solution)/shard_map/ppermute | solution.py:23
  69.2 13.9 %collective-permute-start.11 = (f32[2,1,768]{2,1,0:T(1,128)S(1)}, f32[2,1,768]{2,1,0:T(1,128)S(1)}, u32[]{:S(2)}, u32[]{:S(2)}) collective-permute-start(f32[2,1,768]{2,1,0:T(1,128)S(1)} %get-tuple-element.119), channel_id=1, source_target_pairs={{0,1},{1,2},{2,3},{3,4},{4,5},{5,6},{6,7},{7,8},{8,9},{9,10},{10,1... | collective-permute-start | bytes 18440 | tf_op jit(solution)/shard_map/ppermute | solution.py:23
  71.2 11.9 %collective-permute-start.10 = (f32[2,1,768]{2,1,0:T(1,128)S(1)}, f32[2,1,768]{2,1,0:T(1,128)S(1)}, u32[]{:S(2)}, u32[]{:S(2)}) collective-permute-start(f32[2,1,768]{2,1,0:T(1,128)S(1)} %get-tuple-element.118), channel_id=1, source_target_pairs={{1,0},{2,1},{3,2},{4,3},{5,4},{6,5},{7,6},{8,7},{9,8},{10,9},{11,1... | collective-permute-start | bytes 18440 | tf_op jit(solution)/shard_map/ppermute | solution.py:26
  75.8 3.7 %collective-permute-start.13 = (f32[2,6,1]{2,1,0:T(8,128)S(1)}, f32[2,6,1]{2,1,0:T(8,128)S(1)}, u32[]{:S(2)}, u32[]{:S(2)}) collective-permute-start(f32[2,6,1]{2,1,0:T(8,128)S(1)} %get-tuple-element.121), channel_id=1, source_target_pairs={{0,16},{16,0},{1,17},{17,1},{2,18},{18,2},{3,19},{19,3},{4,20},{20... | collective-permute-start | bytes 152 | tf_op jit(solution)/shard_map/ppermute | solution.py:23
  79.5 3.7 %collective-permute-start.12 = (f32[2,6,1]{2,1,0:T(8,128)S(1)}, f32[2,6,1]{2,1,0:T(8,128)S(1)}, u32[]{:S(2)}, u32[]{:S(2)}) collective-permute-start(f32[2,6,1]{2,1,0:T(8,128)S(1)} %get-tuple-element.120), channel_id=1, source_target_pairs={{16,0},{0,16},{17,1},{1,17},{18,2},{2,18},{19,3},{3,19},{20,4},{4,... | collective-permute-start | bytes 152 | tf_op jit(solution)/shard_map/ppermute | solution.py:26
  88.8 6.5 %collective-permute-start.15 = (f32[2,3,1536]{2,1,0:T(4,128)S(1)}, f32[2,3,1536]{2,1,0:T(4,128)S(1)}, u32[]{:S(2)}, u32[]{:S(2)}) collective-permute-start(f32[2,3,1536]{2,1,0:T(4,128)S(1)} %get-tuple-element.107), channel_id=1, source_target_pairs={{1,0},{2,1},{3,2},{4,3},{5,4},{6,5},{7,6},{8,7},{9,8},{10,9},{11,1... | collective-permute-start | bytes 110600 | tf_op jit(solution)/shard_map/ppermute | solution.py:26
  90.7 8.9 %collective-permute-start.14 = (f32[2,3,1536]{2,1,0:T(4,128)S(1)}, f32[2,3,1536]{2,1,0:T(4,128)S(1)}, u32[]{:S(2)}, u32[]{:S(2)}) collective-permute-start(f32[2,3,1536]{2,1,0:T(4,128)S(1)} %get-tuple-element.106), channel_id=1, source_target_pairs={{0,1},{1,2},{2,3},{3,4},{4,5},{5,6},{6,7},{7,8},{8,9},{9,10},{10,1... | collective-permute-start | bytes 110600 | tf_op jit(solution)/shard_map/ppermute | solution.py:23
  93.2 34.4 %collective-permute-start.17 = (f32[2,1,768]{2,1,0:T(1,128)S(1)}, f32[2,1,768]{2,1,0:T(1,128)S(1)}, u32[]{:S(2)}, u32[]{:S(2)}) collective-permute-start(f32[2,1,768]{2,1,0:T(1,128)S(1)} %get-tuple-element.115), channel_id=1, source_target_pairs={{0,1},{1,2},{2,3},{3,4},{4,5},{5,6},{6,7},{7,8},{8,9},{9,10},{10,1... | collective-permute-start | bytes 18440 | tf_op jit(solution)/shard_map/ppermute | solution.py:23
  95.3 32.2 %collective-permute-start.16 = (f32[2,1,768]{2,1,0:T(1,128)S(1)}, f32[2,1,768]{2,1,0:T(1,128)S(1)}, u32[]{:S(2)}, u32[]{:S(2)}) collective-permute-start(f32[2,1,768]{2,1,0:T(1,128)S(1)} %get-tuple-element.114), channel_id=1, source_target_pairs={{1,0},{2,1},{3,2},{4,3},{5,4},{6,5},{7,6},{8,7},{9,8},{10,9},{11,1... | collective-permute-start | bytes 18440 | tf_op jit(solution)/shard_map/ppermute | solution.py:26
  123.3 3.7 %collective-permute-start.19 = (f32[2,6,1]{2,1,0:T(8,128)S(1)}, f32[2,6,1]{2,1,0:T(8,128)S(1)}, u32[]{:S(2)}, u32[]{:S(2)}) collective-permute-start(f32[2,6,1]{2,1,0:T(8,128)S(1)} %get-tuple-element.117), channel_id=1, source_target_pairs={{0,16},{16,0},{1,17},{17,1},{2,18},{18,2},{3,19},{19,3},{4,20},{20... | collective-permute-start | bytes 152 | tf_op jit(solution)/shard_map/ppermute | solution.py:23
  133.4 10.8 %collective-permute-start.21 = (f32[2,1,768]{2,1,0:T(1,128)S(1)}, f32[2,1,768]{2,1,0:T(1,128)S(1)}, u32[]{:S(2)}, u32[]{:S(2)}) collective-permute-start(f32[2,1,768]{2,1,0:T(1,128)S(1)} %get-tuple-element.111), channel_id=1, source_target_pairs={{0,1},{1,2},{2,3},{3,4},{4,5},{5,6},{6,7},{7,8},{8,9},{9,10},{10,1... | collective-permute-start | bytes 18440 | tf_op jit(solution)/shard_map/ppermute | solution.py:23
  135.4 8.8 %collective-permute-start.20 = (f32[2,1,768]{2,1,0:T(1,128)S(1)}, f32[2,1,768]{2,1,0:T(1,128)S(1)}, u32[]{:S(2)}, u32[]{:S(2)}) collective-permute-start(f32[2,1,768]{2,1,0:T(1,128)S(1)} %get-tuple-element.110), channel_id=1, source_target_pairs={{1,0},{2,1},{3,2},{4,3},{5,4},{6,5},{7,6},{8,7},{9,8},{10,9},{11,1... | collective-permute-start | bytes 18440 | tf_op jit(solution)/shard_map/ppermute | solution.py:26
  140.0 3.7 %collective-permute-start.23 = (f32[2,6,1]{2,1,0:T(8,128)S(1)}, f32[2,6,1]{2,1,0:T(8,128)S(1)}, u32[]{:S(2)}, u32[]{:S(2)}) collective-permute-start(f32[2,6,1]{2,1,0:T(8,128)S(1)} %get-tuple-element.113), channel_id=1, source_target_pairs={{0,16},{16,0},{1,17},{17,1},{2,18},{18,2},{3,19},{19,3},{4,20},{20... | collective-permute-start | bytes 152 | tf_op jit(solution)/shard_map/ppermute | solution.py:23
  (14 other events, 177.2 us)
Sparse Core Ops, SparseCore 0:
  58.1 10.1 reduce-scatter.2
  123.4 9.0 reduce-scatter.4
where the time goes:
time: 153 us
  starting transfers between devices  54.8 us (36%)
  local copies, waits for them, and re-layouts  21.9 us (14%)
  matrix products  20.7 us (14%)
  waiting for transfers between devices  20.6 us (13%)
  between operations  14.9 us (10%)
  other arithmetic  10.2 us (7%)
  blocking collectives  9.4 us (6%)
    ppermute x12, starting transfers between devices, with_halo(): lax.ppermute(lax.slice_in_dim(block, 0, width, axis=dim), axis, backward)  35.1 us
    dot_general x6, matrix products, atmos_step(): jnp.einsum('kl,fmlrn->fmkrn', level_mix, advected, precision=lax.Precisio...  20.5 us
    ppermute x12, starting transfers between devices, with_halo(): lax.ppermute(lax.slice_in_dim(block, block.shape[dim] - width, None, axis...  19.6 us
    scatter x6, local copies, waits for them, and re-layouts, atmos_step(): return mixed_state.at[:, :, 0].set(bottom)  11.2 us
    reduce_scatter x2, waiting for transfers between devices, body(): lax.psum_scatter(flux_terms, 'member', scatter_dimension=2, tiled=True)  10 us
    all_gather x2, blocking collectives, body(): surface = lax.all_gather(ocean, 'member', axis=2, tiled=True)  9.4 us
    ppermute x12, waiting for transfers between devices, with_halo(): lax.ppermute(lax.slice_in_dim(block, block.shape[dim] - width, None, axis...  6.39 us
    ppermute x12, waiting for transfers between devices, with_halo(): lax.ppermute(lax.slice_in_dim(block, 0, width, axis=dim), axis, backward)  4.21 us
  transfers between devices with their start and end apart: 26, of which 8 were waited for; matrix products, arithmetic and copies ran while one was open for 30% of the time, Pallas kernels for 0%

commit v1 on v0

v1 whole, which is shorter than its diff:
```python
import functools

import jax
import jax.numpy as jnp
from jax import lax
from jax.experimental import pallas as pl
from jax.experimental.pallas import tpu as pltpu
from jax.sharding import PartitionSpec as P

ASTEPS = 3
OSTEPS = 2
COUPLE = 2

ADVECTION = 0.1
OCEAN_GAIN = 0.5
OCEAN_DIFFUSION = 0.15

ANY = pl.BlockSpec(memory_space=pl.ANY)
VMEM = pl.BlockSpec(memory_space=pltpu.VMEM)
SMEM = pl.BlockSpec(memory_space=pltpu.SMEM)
LANES = 128


def place(up, row, base, count):
    return jnp.where(up == 1, row - base, count - 1 - (row - base))


def chunk(up, row, length, base, count):
    return jnp.where(up == 1, row - base, count - length - (row - base))


class Sems:
    def __init__(self, sems):
        self.sems, self.used = sems, 0

    def copies(self):
        return Group(self)


class Group:
    def __init__(self, owner):
        self.owner, self.started = owner, []

    def start(self, source, target):
        copy = pltpu.make_async_copy(source, target, self.owner.sems.at[self.owner.used])
        self.owner.used += 1
        copy.start()
        self.started.append(copy)

    def wait(self):
        for copy in self.started:
            copy.wait()


def atmos_rows(up, reals, coef, source, target, surface, first, count, edge, valid):
    src, src_base, src_rows = source
    dst, dst_base, dst_rows = target
    srf, srf_base, srf_rows = surface
    members, lon = src.shape[1], src.shape[4]
    level = lax.broadcasted_iota(jnp.int32, (8, LANES), 0)

    def one(i, carry):
        row = first + i
        here = place(up, row, src_base, src_rows)
        there = place(up, row, dst_base, dst_rows)
        sea = place(up, row, srf_base, srf_rows)
        for m in range(members):
            diffusivity = reals[m]
            keep = 1.0 - 4.0 * diffusivity
            wind = None
            for c in (1, 0):
                centre = src[c, m, here]
                if wind is None:
                    wind = (0.5 * ADVECTION) * centre
                eastern = pltpu.roll(centre, lon - 1, 1)
                western = pltpu.roll(centre, 1, 1)
                beside = src[c, m, here - 1] + src[c, m, here + 1]
                advected = (
                    keep * centre
                    + diffusivity * (beside + (eastern + western))
                    - wind * (eastern - western)
                )
                relax = jnp.where(level == 0, reals[members + c * members + m], 0.0)
                for t in range(lon // LANES):
                    part = advected[:, t * LANES : (t + 1) * LANES]
                    total = coef[c, m, 0] * part
                    for d in range(1, 8):
                        total += coef[c, m, d] * pltpu.roll(part, 8 - d, 0)
                    total += relax * srf[sea, c : c + 1, t * LANES : (t + 1) * LANES]
                    if edge is not None:
                        total = total * jnp.where(row >= edge, valid, 1.0)
                    dst[c, m, there, :, t * LANES : (t + 1) * LANES] = total
        return carry

    lax.fori_loop(0, count, one, 0)


def flux_rows(up, reals, state, surface, out, first, count, ensemble):
    st, st_base, st_rows = state
    srf, srf_base, srf_rows = surface
    ref, base, rows = out
    members = st.shape[1]

    def one(i, carry):
        row = first + i
        at = place(up, row, st_base, st_rows)
        sea = place(up, row, srf_base, srf_rows)
        to = place(up, row, base, rows)
        for c in range(2):
            s = srf[sea, c : c + 1, :]
            flux = jnp.zeros_like(s)
            for m in range(members):
                flux += reals[members + c * members + m] * (st[c, m, at, 0:1, :] - s)
            ref[to, c : c + 1, :] = flux * (1.0 / ensemble)
        return carry

    lax.fori_loop(0, count, one, 0)


def ocean_rows(up, sea, ocean, forcing, target, first, count):
    src, src_base, src_rows = ocean
    fixed, fixed_base, fixed_rows = sea
    frc, frc_base, frc_rows = forcing
    dst, dst_base, dst_rows = target
    lon = src.shape[2]

    def one(i, carry):
        row = first + i
        here = place(up, row, src_base, src_rows)
        cell = place(up, row, fixed_base, fixed_rows)
        force = place(up, row, frc_base, frc_rows)
        to = place(up, row, dst_base, dst_rows)
        mask = fixed[cell, 3:4, :]
        for c in range(2):
            centre = src[here, c : c + 1, :]
            laplace = (
                (pltpu.roll(centre, lon - 1, 1) + pltpu.roll(centre, 1, 1))
                + (src[here - 1, c : c + 1, :] + src[here + 1, c : c + 1, :])
                - 4.0 * centre
            )
            rate = OCEAN_DIFFUSION if c == 0 else fixed[cell, 2:3, :]
            dst[to, c : c + 1, :] = centre + mask * (OCEAN_GAIN * frc[force, c : c + 1, :] + rate * laplace)
        return carry

    lax.fori_loop(0, count, one, 0)


def load_three(up, group, target, band, low, own, high):
    group.start(low, target.at[pl.ds(jnp.where(up == 1, 0, 2 * band), band)])
    group.start(own, target.at[pl.ds(band, band)])
    group.start(high, target.at[pl.ds(jnp.where(up == 1, 2 * band, 0), band)])


def inner_kernel(cfg, coupled, *refs):
    band, H, ensemble = cfg
    refs = list(refs)
    sems = refs.pop()
    ints, reals, coef, a_low, a_in, a_out, sea_low, sea_own, sea_high = refs[:9]
    del refs[:9]
    if coupled:
        f_low, f_own, f_high = refs[:3]
        del refs[:3]
        done, carry1, carry2, flux, surface_out = refs[:5]
        del refs[:5]
    else:
        done, carry1, carry2, flux = refs[:4]
        del refs[:4]
    win, lev1, lev2, sea = refs[:4]
    del refs[:4]
    up = ints[0]
    pool = Sems(sems)
    loads = pool.copies()
    size = 3 * H
    loads.start(a_low, win.at[:, :, pl.ds(chunk(up, -H, H, -H, size), H)])
    loads.start(a_in, win.at[:, :, pl.ds(chunk(up, 0, H, -H, size), H)])
    loads.start(a_out, win.at[:, :, pl.ds(chunk(up, H, H, -H, size), H)])
    load_three(up, loads, sea, band, sea_low, sea_own, sea_high)
    whole = 3 * band
    if coupled:
        force, middle, surf = refs
        load_three(up, loads, force, band, f_low, f_own, f_high)
    loads.wait()
    fixed = (sea, -band, whole)
    if coupled:
        forcing, half = (force, -band, whole), (middle, -band, whole)
        ocean_rows(up, fixed, fixed, forcing, half, -H, 2 * H + 3)
        surface = (surf, -band, whole)
        ocean_rows(up, fixed, half, forcing, surface, -H + 1, 2 * H + 1)
    else:
        surface = fixed
    step0, step1, step2 = (win, -H, size), (lev1, 1 - H, 7), (lev2, 2 - H, 5)
    step3 = (done, 0, H)
    atmos_rows(up, reals, coef, step0, step1, surface, 1 - H, 7, None, None)
    atmos_rows(up, reals, coef, step1, step2, surface, 2 - H, 5, None, None)
    atmos_rows(up, reals, coef, step2, step3, surface, 0, 3, None, None)
    stores = pool.copies()
    stores.start(lev1.at[:, :, pl.ds(chunk(up, 3, 2, 1 - H, 7), 2)], carry1)
    stores.start(lev2.at[:, :, pl.ds(chunk(up, 2, 2, 2 - H, 5), 2)], carry2)
    if coupled:
        stores.start(surf, surface_out)
    flux_rows(up, reals, step3, surface, (flux, 0, H), 0, H, ensemble)
    stores.wait()


def tile(up, reals, coef, win, lev1, lev2, target, base, surface, edge, valid):
    atmos_rows(up, reals, coef, (win, base - 1, 5), (lev1, base - 2, 5), surface, base, 3, edge, valid)
    atmos_rows(up, reals, coef, (lev1, base - 2, 5), (lev2, base - 3, 5), surface, base - 1, 3, edge, valid)
    atmos_rows(up, reals, coef, (lev2, base - 3, 5), target, surface, base - 2, 3, edge, valid)


def outer_kernel(cfg, ints, reals, coef, a_out, a_high, carry1, carry2, flux_in, sea_low, sea_own, sea_high,
                 done, next1, next2, flux, win, lev1, lev2, sea, sems):
    band, H, ensemble = cfg
    up, valid = ints[0], reals[reals.shape[0] - 1]
    pool = Sems(sems)
    loads = pool.copies()
    loads.start(a_out.at[:, :, pl.ds(chunk(up, 4, 2, 3, 3), 2)], win.at[:, :, pl.ds(chunk(up, 4, 2, 4, 5), 2)])
    loads.start(a_high, win.at[:, :, pl.ds(chunk(up, 6, 3, 4, 5), 3)])
    loads.start(carry1, lev1.at[:, :, pl.ds(chunk(up, 3, 2, 3, 5), 2)])
    loads.start(carry2, lev2.at[:, :, pl.ds(chunk(up, 2, 2, 2, 5), 2)])
    load_three(up, loads, sea, band, sea_low, sea_own, sea_high)
    loads.start(flux_in, flux.at[pl.ds(chunk(up, 0, H, 0, band), H)])
    loads.wait()
    surface = (sea, -band, 3 * band)
    tile(up, reals, coef, win, lev1, lev2, (done, 3, 3), 5, surface, band, valid)
    stores = pool.copies()
    stores.start(lev1.at[:, :, pl.ds(chunk(up, 6, 2, 3, 5), 2)], next1)
    stores.start(lev2.at[:, :, pl.ds(chunk(up, 5, 2, 2, 5), 2)], next2)
    flux_rows(up, reals, (done, 3, 3), surface, (flux, 0, band), 3, 3, ensemble)
    stores.wait()


def last_kernel(cfg, ints, reals, coef, a_high, a_far, carry1, carry2, sea_low, sea_own, sea_high,
                f_low, f_own, f_high, b_out, b_in, b_carry1, b_carry2, flux_in,
                result, flux, surface_out, win, lev1, lev2, win_b, lev1_b, lev2_b, done, sea, force, middle, surf, sems):
    band, H, ensemble = cfg
    up, valid = ints[0], reals[reals.shape[0] - 1]
    pool = Sems(sems)
    loads = pool.copies()
    whole = 3 * band
    loads.start(a_high.at[:, :, pl.ds(chunk(up, 7, 2, 6, 3), 2)], win.at[:, :, pl.ds(chunk(up, 7, 2, 7, 5), 2)])
    loads.start(a_far, win.at[:, :, pl.ds(chunk(up, 9, 3, 7, 5), 3)])
    loads.start(carry1, lev1.at[:, :, pl.ds(chunk(up, 6, 2, 6, 5), 2)])
    loads.start(carry2, lev2.at[:, :, pl.ds(chunk(up, 5, 2, 5, 5), 2)])
    load_three(up, loads, sea, band, sea_low, sea_own, sea_high)
    load_three(up, loads, force, band, f_low, f_own, f_high)
    loads.start(b_out.at[:, :, pl.ds(chunk(up, 4, 2, 3, 3), 2)], win_b.at[:, :, pl.ds(chunk(up, 4, 2, 4, 5), 2)])
    loads.start(b_carry1, lev1_b.at[:, :, pl.ds(chunk(up, 3, 2, 3, 5), 2)])
    loads.start(b_carry2, lev2_b.at[:, :, pl.ds(chunk(up, 2, 2, 2, 5), 2)])
    loads.start(flux_in, flux.at[pl.ds(chunk(up, 0, H, 0, band), H)])
    loads.wait()
    stores = pool.copies()
    stores.start(b_in, result.at[:, :, pl.ds(chunk(up, 0, H, 0, band), H)])
    fixed, forcing, half = (sea, -band, whole), (force, -band, whole), (middle, -band, whole)
    surface = (surf, -band, whole)
    ocean_rows(up, fixed, fixed, forcing, half, -3, 12)
    ocean_rows(up, fixed, half, forcing, surface, -2, 10)
    tile(up, reals, coef, win, lev1, lev2, (win_b, 4, 5), 8, fixed, band, valid)
    tile(up, reals, coef, win_b, lev1_b, lev2_b, (done, 3, 3), 5, surface, band, valid)
    stores.start(done, result.at[:, :, pl.ds(chunk(up, 3, H, 0, band), H)])
    stores.start(surf, surface_out)
    flux_rows(up, reals, (done, 3, 3), surface, (flux, 0, band), 3, 3, ensemble)
    stores.wait()


def ocean_kernel(cfg, ints, surface_in, sea_low, sea_own, sea_high, f_low, f_own, f_high, out,
                 sea, surf, force, middle, final, sems):
    band, H, tile_width = cfg
    up = ints[0]
    pool = Sems(sems)
    loads = pool.copies()
    whole = 3 * band
    load_three(up, loads, sea, band, sea_low, sea_own, sea_high)
    loads.start(surface_in, surf)
    loads.start(f_low, force.at[pl.ds(chunk(up, -1, 1, -1, band + 2), 1)])
    loads.start(f_own, force.at[pl.ds(1, band)])
    loads.start(f_high, force.at[pl.ds(chunk(up, band, 1, -1, band + 2), 1)])
    loads.wait()
    fixed, ocean = (sea, -band, whole), (surf, -band, whole)
    forcing, half = (force, -1, band + 2), (middle, -1, band + 2)
    ocean_rows(up, fixed, ocean, forcing, half, -1, band + 2)
    ocean_rows(up, fixed, half, forcing, (final, 0, band), 0, band)
    if tile_width is None:
        out[...] = final[...]
    else:
        out[...] = final[:, :, pl.ds(pl.multiple_of(ints[1] * tile_width, LANES), tile_width)]


def call(kernel, name, outs, scratch, args, copies, flops=0):
    kinds = {"any": ANY, "vmem": VMEM, "smem": SMEM}
    return pl.pallas_call(
        kernel,
        name=name,
        out_shape=[jax.ShapeDtypeStruct(shape, jnp.float32) for _, shape in outs],
        in_specs=[kinds[kind] for kind, _ in args],
        out_specs=[kinds[kind] for kind, _ in outs],
        scratch_shapes=[pltpu.VMEM(shape, jnp.float32) for shape in scratch] + [pltpu.SemaphoreType.DMA((copies,))],
        compiler_params=pltpu.CompilerParams(vmem_limit_bytes=24 * 1024 * 1024),
        cost_estimate=pl.CostEstimate(flops=flops, bytes_accessed=4 * 1024 * 1024, transcendentals=0),
    )(*[value for _, value in args])


def lookup(parameter_index, parameter_table):
    onehot = (
        parameter_index[:, None] == jnp.arange(parameter_table.shape[0], dtype=jnp.int32)[None, :]
    ).astype(jnp.float32)
    picked = jnp.dot(
        onehot, parameter_table, precision=lax.Precision.HIGHEST, preferred_element_type=jnp.float32
    )
    return (0.6 * picked[:, 0], 2.0 * jnp.transpose(picked[:, 1:3]))


def mixing(level_mix, exchange):
    levels = level_mix.shape[0]
    ids = jnp.arange(levels)
    pick = (ids[None, None, :] == (ids[None, :, None] + ids[:, None, None]) % levels).astype(jnp.float32)
    whole = level_mix + jnp.eye(levels, dtype=jnp.float32)
    turned = jnp.sum(pick * whole[None], axis=2)
    scale = jnp.where(ids == 0, 1.0 - exchange[:, :, None], 1.0)
    coef = turned[None, None] * scale[:, :, None, :]
    return jnp.broadcast_to(coef[..., None], coef.shape + (LANES,))


def body(atmosphere, ocean_state, viscosity, sea_mask, parameter_index, parameter_table, level_mix):
    H = ASTEPS
    fields, members, levels, band, lon = atmosphere.shape
    width = ocean_state.shape[2]
    sides, bands = lax.axis_size("member"), lax.axis_size("lat")
    ensemble = members * sides
    position = lax.axis_index("lat")
    side = lax.axis_index("member")
    up = position % 2
    near = [(i, i + 1) for i in range(0, bands, 2)]
    near += [(b, a) for a, b in near]
    far = [(i, i + 1) for i in range(1, bands - 1, 2)]
    far += [(b, a) for a, b in far]
    other = [(0, 1), (1, 0)]

    def to_near(x):
        return lax.ppermute(x, "lat", near)

    def to_far(x):
        return lax.ppermute(x, "lat", far)

    def total(x):
        if sides == 2:
            return x + lax.ppermute(x, "member", other)
        return lax.psum(x, "member")

    def full_rows(x):
        if sides == 2:
            y = lax.ppermute(x, "member", other)
            low, high = jnp.where(side == 0, x, y), jnp.where(side == 0, y, x)
            return jnp.concatenate([low, high], axis=2)
        return lax.all_gather(x, "member", axis=2, tiled=True)

    state = jnp.transpose(atmosphere, (0, 1, 3, 2, 4))
    a_out = lax.dynamic_slice_in_dim(state, up * H, H, 2)
    a_high = to_far(a_out)
    a_in = lax.dynamic_slice_in_dim(state, (1 - up) * H, H, 2)
    a_low = to_near(a_in)

    tile_fields = jnp.concatenate([jnp.transpose(ocean_state, (1, 0, 2)), viscosity[:, None]], axis=1)
    sea_own = jnp.concatenate([full_rows(tile_fields), sea_mask.astype(jnp.float32)[:, None]], axis=1)
    sea_low, sea_high = to_near(sea_own), to_far(sea_own)

    diffusivity, exchange = lookup(parameter_index, parameter_table)
    coef = mixing(level_mix, exchange)
    valid = jnp.where(up == 1, position < bands - 1, position > 0).astype(jnp.float32)
    reals = jnp.concatenate([diffusivity, exchange.reshape(-1), valid[None]])
    ints = jnp.stack([up, side]).astype(jnp.int32)
    common = [("smem", ints), ("smem", reals), ("vmem", coef)]
    seas = [("any", sea_low), ("any", sea_own), ("any", sea_high)]

    def rows(n):
        return (fields, members, n, levels, lon)

    cfg = (band, H, ensemble)
    unit = members * fields * levels * lon * 30

    def inner(coupled, low, inside, outside, sea3, force3, name):
        outs = [("vmem", rows(H)), ("any", rows(2)), ("any", rows(2)), ("vmem", (H, fields, lon))]
        scratch = [rows(3 * H), rows(7), rows(5), (3 * band, 4, lon)]
        if coupled:
            scratch += [(3 * band, 2, lon)] * 3
            outs += [("any", (3 * band, 2, lon))]
        args = common + [("any", low), ("any", inside), ("any", outside)] + sea3 + force3
        return call(functools.partial(inner_kernel, cfg, coupled), name, outs, scratch, args, 16, 15 * unit)

    b_in, carry1, carry2, flux = inner(False, a_low, a_in, a_out, seas[:2] + [("any", sea_own)], [], "inner_first")
    a_far = to_far(a_in)
    b_low = to_near(b_in)
    b_out, carry1, carry2, flux = call(
        functools.partial(outer_kernel, cfg), "outer_first",
        [("vmem", rows(H)), ("any", rows(2)), ("any", rows(2)), ("vmem", (band, fields, lon))],
        [rows(5), rows(5), rows(5), (3 * band, 4, lon)],
        common + [("any", a_out), ("any", a_high), ("any", carry1), ("any", carry2), ("any", flux)] + seas, 16, 9 * unit)
    f_own = total(flux)
    f_low, f_high = to_near(f_own), to_far(f_own)
    c_in, b_carry1, b_carry2, flux, _ = inner(
        True, b_low, b_in, b_out, seas,
        [("any", f_low), ("any", f_own), ("any", f_own)], "inner_second")
    result, flux, surface = call(
        functools.partial(last_kernel, cfg), "outer_second",
        [("any", rows(band)), ("vmem", (band, fields, lon)), ("any", (3 * band, 2, lon))],
        [rows(5)] * 6 + [rows(H), (3 * band, 4, lon)] + [(3 * band, 2, lon)] * 3,
        common + [("any", a_high), ("any", a_far), ("any", carry1), ("any", carry2)] + seas
        + [("any", f_low), ("any", f_own), ("any", f_high), ("any", b_out), ("any", c_in), ("any", b_carry1), ("any", b_carry2), ("any", flux)],
        24, 18 * unit)
    g_own = total(flux)
    g_low = to_near(lax.dynamic_slice_in_dim(g_own, (1 - up) * (band - 1), 1, 0))
    g_high = to_far(lax.dynamic_slice_in_dim(g_own, up * (band - 1), 1, 0))
    inside_kernel = width % LANES == 0
    (ocean,) = call(
        functools.partial(ocean_kernel, (band, H, width if inside_kernel else None)), "ocean_last",
        [("vmem", (band, fields, width if inside_kernel else lon))],
        [(3 * band, 4, lon), (3 * band, 2, lon), (band + 2, 2, lon), (band + 2, 2, lon), (band, 2, lon)],
        [("smem", ints), ("any", surface)] + seas + [("any", g_low), ("any", g_own), ("any", g_high)], 8)
    if not inside_kernel:
        ocean = lax.dynamic_slice_in_dim(ocean, side * width, width, 2)
    return (jnp.transpose(result, (0, 1, 3, 2, 4)), jnp.transpose(ocean, (1, 0, 2)))


def solution(mesh):
    return jax.shard_map(
        body,
        mesh=mesh,
        in_specs=(
            P(None, "member", None, "lat", None),
            P(None, "lat", "member"),
            P("lat", "member"),
            P("lat", None),
            P("member"),
            P(),
            P(),
        ),
        out_specs=(P(None, "member", None, "lat", None), P(None, "lat", "member")),
        check_vma=False,
    )
```

time: 153 us -> 86.7 us (0.57)
  Pallas kernels: 0 us -> 35.6 us
  starting transfers between devices: 54.8 us -> 26.5 us
  matrix products: 20.7 us -> 0.18 us
  local copies, waits for them, and re-layouts: 21.9 us -> 2.56 us
  between operations: 14.9 us -> 0.89 us
  blocking collectives: 9.4 us -> 0 us
  other arithmetic: 10.2 us -> 1.68 us
  waiting for transfers between devices: 20.6 us -> 18.9 us
    pallas_call x0 -> x5, Pallas kernels: none -> 35.6 us  [call(): pl.pallas_call(kernel, name=name, out_shape=[jax.ShapeDtypeStruct(shape,...]
    ppermute x24 -> x13, starting transfers between devices: 54.8 us -> 26.5 us  [the longest x5 16.2 us: to_far(): return lax.ppermute(x, 'lat', far)]
    dot_general x6 -> x0, matrix products: 20.5 us -> none  [atmos_step(): jnp.einsum('kl,fmlrn->fmkrn', level_mix, advected, precision=lax.Precisio...]
    scatter x6 -> x0, local copies, waits for them, and re-layouts: 11.2 us -> none  [atmos_step(): return mixed_state.at[:, :, 0].set(bottom)]
    reduce_scatter x2 -> x0, waiting for transfers between devices: 10 us -> none  [body(): lax.psum_scatter(flux_terms, 'member', scatter_dimension=2, tiled=True)]
    all_gather x2 -> x0, blocking collectives: 9.4 us -> none  [body(): surface = lax.all_gather(ocean, 'member', axis=2, tiled=True)]
    ppermute x24 -> x13, waiting for transfers between devices: 10.6 us -> 18.9 us  [the longest x5 10.3 us: to_far(): return lax.ppermute(x, 'lat', far)]
    slice x33 -> x0, local copies, waits for them, and re-layouts: 7.73 us -> none  [the longest x10 3.13 us: atmos_step(): eastern = jnp.roll(centre, -1, axis=4)]
  transfers between devices with their start and end apart: 26 -> 13, of which waited for: 8 -> 5; matrix products, arithmetic and copies ran while one was open for 30% -> 3% of each run, Pallas kernels for 0% -> 23%
where the time goes in v1:
time: 86.7 us; the launch traced here: 86.3 us
  Pallas kernels  35.6 us (41%)
  starting transfers between devices  26.5 us (31%)
  waiting for transfers between devices  18.9 us (22%)
  local copies, waits for them, and re-layouts  2.56 us (3%)
  other arithmetic  1.68 us (2%)
  between operations  0.89 us (1%)
    pallas_call x5, Pallas kernels, call(): pl.pallas_call(kernel, name=name, out_shape=[jax.ShapeDtypeStruct(shape,...  35.6 us
    ppermute x5, starting transfers between devices, to_far(): return lax.ppermute(x, 'lat', far)  16.2 us
    ppermute x5, waiting for transfers between devices, to_far(): return lax.ppermute(x, 'lat', far)  10.3 us
    ppermute x2, waiting for transfers between devices, total(): return x + lax.ppermute(x, 'member', other)  7.64 us
    ppermute x5, starting transfers between devices, to_near(): return lax.ppermute(x, 'lat', near)  7.59 us
  transfers between devices with their start and end apart: 13, of which 5 were waited for; matrix products, arithmetic and copies ran while one was open for 3% of the time, Pallas kernels for 23%

profile of v1, /device:TPU:8, one launch (start us, length us, event | category | flops | bytes accessed | tf_op | source)
XLA Modules:
  0.0 86.3 jit_solution(2424731032219975431)
XLA Ops:
  0.6 0.8 broadcast_in_dim.49
  1.4 0.8 pad_maximum_fusion.1
  2.2 1.6 %collective-permute-start.3 = (f32[6,3,768]{2,1,0:T(4,128)S(1)}, f32[6,3,768]{2,1,0:T(4,128)S(1)}, u32[]{:S(2)}, u32[]{:S(2)}) collective-permute-start(f32[6,3,768]{2,1,0:T(4,128)S(1)} %pad_maximum_fusion.1), channel_id=1, source_target_pairs={{0,16},{16,0},{1,17},{17,1},{2,18},{18,2},{3,19},{19,3},{4,20},{20... | collective-permute-start | bytes 165896 | tf_op jit(solution)/shard_map/ppermute | solution.py:352
  3.8 1.4 %dynamic-slice_bitcast_fusion = (f32[2,2,3,8,1536]{4,3,2,1,0:T(8,128)S(1)}, f32[2,2,3,8,1536]{4,3,2,1,0:T(8,128)S(1)}) fusion(f32[2,2,8,6,1536]{4,2,3,1,0:T(8,128)} %param.7, s32[]{:T(128)S(6)} %select_n.59, s32[]{:T(128)S(6)} %select_n.58), kind=kLoop, calls=%fused_computation | loop fusion | bytes 2359304 | tf_op jit(solution)/shard_map/dynamic_slice | solution.py:360
  5.2 3.4 %collective-permute-start = (f32[2,2,3,8,1536]{4,3,2,1,0:T(8,128)S(1)}, f32[2,2,3,8,1536]{4,3,2,1,0:T(8,128)S(1)}, u32[]{:S(2)}, u32[]{:S(2)}) collective-permute-start(f32[2,2,3,8,1536]{4,3,2,1,0:T(8,128)S(1)} %get-tuple-element.33.refs_5_.a_out), channel_id=1, source_target_pairs={{1,2},{3,4},{5,6},{7,8},{9,10},{11,12},{13,14},{2,1},{4,3},{6,5},{... | collective-permute-start | bytes 1769480 | tf_op jit(solution)/shard_map/ppermute | solution.py:343
  10.2 0.9 %collective-permute-done.4.refs_6_.sea_low = f32[6,4,1536]{2,1,0:T(4,128)S(1)} collective-permute-done((f32[6,4,1536]{2,1,0:T(4,128)S(1)}, f32[6,4,1536]{2,1,0:T(4,128)S(1)}, u32[]{:S(2)}, u32[]{:S(2)}) %collective-permute-start.4) | collective-permute-done | bytes 147488 | tf_op jit(solution)/shard_map/ppermute | solution.py:340
  11.2 6.2 %inner_first.1 = (f32[2,2,3,8,1536]{4,3,2,1,0:T(8,128)S(1)}, f32[2,2,2,8,1536]{4,3,2,1,0:T(8,128)S(1)}, f32[2,2,2,8,1536]{4,3,2,1,0:T(8,128)S(1)}, f32[3,2,1536]{2,1,0:T(2,128)S(1)}) custom-call(s32[2]{0:T(128)S(1)} %pad_add_fusion.refs_0_.ints, f32[7]{0:T(128)S(1)} %pad_maximum_fusion.2.refs_1_.reals, ...), custom_call_target="tpu_custom_call" | custom-call | flops 22118400 | bytes 4194304 | tf_op jit(solution)/shard_map/inner_first/pallas_call | solution.py:291
  17.5 0.2 collective-permute-start.9
  17.7 3.0 %collective-permute-start.1 = (f32[2,2,3,8,1536]{4,3,2,1,0:T(8,128)S(1)}, f32[2,2,3,8,1536]{4,3,2,1,0:T(8,128)S(1)}, u32[]{:S(2)}, u32[]{:S(2)}) collective-permute-start(f32[2,2,3,8,1536]{4,3,2,1,0:T(8,128)S(1)} %get-tuple-element.32.refs_4_), channel_id=1, source_target_pairs={{1,2},{3,4},{5,6},{7,8},{9,10},{11,12},{13,14},{2,1},{4,3},{6,5},{... | collective-permute-start | bytes 1769480 | tf_op jit(solution)/shard_map/ppermute | solution.py:343
  20.8 3.4 %collective-permute-start.5 = (f32[6,4,1536]{2,1,0:T(4,128)S(1)}, f32[6,4,1536]{2,1,0:T(4,128)S(1)}, u32[]{:S(2)}, u32[]{:S(2)}) collective-permute-start(f32[6,4,1536]{2,1,0:T(4,128)S(1)} %pad_maximum_fusion.refs_7_.refs_8_.sea_own), channel_id=1, source_target_pairs={{1,2},{3,4},{5,6},{7,8},{9,10},{11,12},{13,14},{2,1},{4,3},{6,5},{... | collective-permute-start | bytes 442376 | tf_op jit(solution)/shard_map/ppermute | solution.py:343
  24.2 7.3 %collective-permute-done.5.sea_high.refs_8_ = f32[6,4,1536]{2,1,0:T(4,128)S(1)} collective-permute-done((f32[6,4,1536]{2,1,0:T(4,128)S(1)}, f32[6,4,1536]{2,1,0:T(4,128)S(1)}, u32[]{:S(2)}, u32[]{:S(2)}) %collective-permute-start.5) | collective-permute-done | bytes 147488 | tf_op jit(solution)/shard_map/ppermute | solution.py:343
  31.5 4.6 %outer_first.1 = (f32[2,2,3,8,1536]{4,3,2,1,0:T(8,128)S(1)}, f32[2,2,2,8,1536]{4,3,2,1,0:T(8,128)S(1)}, f32[2,2,2,8,1536]{4,3,2,1,0:T(8,128)S(1)}, f32[6,2,1536]{2,1,0:T(2,128)S(1)}) custom-call(s32[2]{0:T(128)S(1)} %pad_add_fusion.refs_0_.ints, f32[7]{0:T(128)S(1)} %pad_maximum_fusion.2.refs_1_.reals, ...), custom_call_target="tpu_custom_call" | custom-call | flops 13271040 | bytes 4194304 | tf_op jit(solution)/shard_map/outer_first/pallas_call | solution.py:291
  36.1 0.6 collective-permute-start.6
  36.7 3.8 %collective-permute-done.6 = f32[6,2,1536]{2,1,0:T(2,128)S(1)} collective-permute-done((f32[6,2,1536]{2,1,0:T(2,128)S(1)}, f32[6,2,1536]{2,1,0:T(2,128)S(1)}, u32[]{:S(2)}, u32[]{:S(2)}) %collective-permute-start.6) | collective-permute-done | bytes 73760 | tf_op jit(solution)/shard_map/ppermute | solution.py:347
  40.5 6.5 %collective-permute-start.7 = (f32[6,2,1536]{2,1,0:T(2,128)S(1)}, f32[6,2,1536]{2,1,0:T(2,128)S(1)}, u32[]{:S(2)}, u32[]{:S(2)}) collective-permute-start(f32[6,2,1536]{2,1,0:T(2,128)S(1)} %add.62.refs_10_.refs_11_.f_own), channel_id=1, source_target_pairs={{0,1},{2,3},{4,5},{6,7},{8,9},{10,11},{12,13},{14,15},{1,0},{3,2},... | collective-permute-start | bytes 221192 | tf_op jit(solution)/shard_map/ppermute | solution.py:340
  47.0 4.1 %collective-permute-start.8 = (f32[6,2,1536]{2,1,0:T(2,128)S(1)}, f32[6,2,1536]{2,1,0:T(2,128)S(1)}, u32[]{:S(2)}, u32[]{:S(2)}) collective-permute-start(f32[6,2,1536]{2,1,0:T(2,128)S(1)} %add.62.refs_10_.refs_11_.f_own), channel_id=1, source_target_pairs={{1,2},{3,4},{5,6},{7,8},{9,10},{11,12},{13,14},{2,1},{4,3},{6,5},{... | collective-permute-start | bytes 221192 | tf_op jit(solution)/shard_map/ppermute | solution.py:343
  51.1 9.3 %inner_second.1 = (f32[2,2,3,8,1536]{4,3,2,1,0:T(8,128)S(1)}, f32[2,2,2,8,1536]{4,3,2,1,0:T(8,128)S(1)}, f32[2,2,2,8,1536]{4,3,2,1,0:T(8,128)S(1)}, f32[3,2,1536]{2,1,0:T(2,128)S(1)}, f32[18,2,1536]{2,1,0:T(2,128)}) custom-call(s32[2]{0:T(128)S(1)} %pad_add_fusion.refs_0_.ints, f32[7]{0:T(128)S(1)} %pad_maximum_fusion.2.refs_1_.reals, ...), custom_call_target="tpu_custom_call" | custom-call | flops 22118400 | bytes 4194304 | tf_op jit(solution)/shard_map/inner_second/pallas_call | solution.py:291
  60.4 11.5 %outer_second.1 = (f32[2,2,6,8,1536]{4,3,2,1,0:T(8,128)}, f32[6,2,1536]{2,1,0:T(2,128)S(1)}, f32[18,2,1536]{2,1,0:T(2,128)S(1)}) custom-call(s32[2]{0:T(128)S(1)} %pad_add_fusion.refs_0_.ints, f32[7]{0:T(128)S(1)} %pad_maximum_fusion.2.refs_1_.reals, f32[2,2,8,8,128]{4,3,2,1,0:T(8,128)S(1)} %broadcast_in_dim.48.refs_2_.coef, ...), custom_call_target="tpu_custom_call" | custom-call | flops 26542080 | bytes 4194304 | tf_op jit(solution)/shard_map/outer_second/pallas_call | solution.py:291
  71.9 0.6 collective-permute-start.10
  72.5 3.8 %collective-permute-done.10 = f32[6,2,1536]{2,1,0:T(2,128)S(1)} collective-permute-done((f32[6,2,1536]{2,1,0:T(2,128)S(1)}, f32[6,2,1536]{2,1,0:T(2,128)S(1)}, u32[]{:S(2)}, u32[]{:S(2)}) %collective-permute-start.10) | collective-permute-done | bytes 73760 | tf_op jit(solution)/shard_map/ppermute | solution.py:347
  76.4 2.3 %collective-permute-start.12 = (f32[1,2,1536]{2,1,0:T(2,128)S(1)}, f32[1,2,1536]{2,1,0:T(2,128)S(1)}, u32[]{:S(2)}, u32[]{:S(2)}) collective-permute-start(f32[1,2,1536]{2,1,0:T(2,128)S(1)} %get-tuple-element.36), channel_id=1, source_target_pairs={{1,2},{3,4},{5,6},{7,8},{9,10},{11,12},{13,14},{2,1},{4,3},{6,5},{... | collective-permute-start | bytes 36872 | tf_op jit(solution)/shard_map/ppermute | solution.py:343
  78.6 0.6 collective-permute-start.11
  79.3 3.0 %collective-permute-done.12.f_high = f32[1,2,1536]{2,1,0:T(2,128)S(1)} collective-permute-done((f32[1,2,1536]{2,1,0:T(2,128)S(1)}, f32[1,2,1536]{2,1,0:T(2,128)S(1)}, u32[]{:S(2)}, u32[]{:S(2)}) %collective-permute-start.12) | collective-permute-done | bytes 12320 | tf_op jit(solution)/shard_map/ppermute | solution.py:343
  82.3 4.0 %ocean_last.1 = f32[6,2,768]{2,1,0:T(2,128)} custom-call(s32[2]{0:T(128)S(1)} %pad_add_fusion.refs_0_.ints, f32[18,2,1536]{2,1,0:T(2,128)S(1)} %get-tuple-element.30.surface_in, f32[6,4,1536]{2,1,0:T(4,128)S(1)} %collective-permute-done.4.refs_6_.sea_low, f32[6,4,1536]{2,1,0:T(4,128)S(1)} %pad_maximum_fusion.refs_7_.refs_8_.sea_own, ...), custom_call_target="tpu_custom_call" | custom-call | bytes 4194304 | tf_op jit(solution)/shard_map/ocean_last/pallas_call | solution.py:291
  (43 shorter events, 1.8 us)
Async XLA Ops:
  0.6 8.0 %copy-start = (f32[32,3]{0,1:T(4,128)S(1)}, f32[32,3]{0,1:T(4,128)}, u32[]{:S(2)}) copy-start(f32[32,3]{0,1:T(4,128)} %param.12) | copy-start | bytes 1156
  2.2 7.3 %collective-permute-start.3 = (f32[6,3,768]{2,1,0:T(4,128)S(1)}, f32[6,3,768]{2,1,0:T(4,128)S(1)}, u32[]{:S(2)}, u32[]{:S(2)}) collective-permute-start(f32[6,3,768]{2,1,0:T(4,128)S(1)} %pad_maximum_fusion.1), channel_id=1, source_target_pairs={{0,16},{16,0},{1,17},{17,1},{2,18},{18,2},{3,19},{19,3},{4,20},{20... | collective-permute-start | bytes 165896 | tf_op jit(solution)/shard_map/ppermute | solution.py:352
  3.8 4.9 %copy-start.4 = (s32[2]{0:T(128)S(1)}, s32[2]{0:T(128)}, u32[]{:S(2)}) copy-start(s32[2]{0:T(128)} %param.11) | copy-start | bytes 28
  3.8 5.3 %copy-start.3 = (f32[8,8]{1,0:T(8,128)S(1)}, f32[8,8]{1,0:T(8,128)}, u32[]{:S(2)}) copy-start(f32[8,8]{1,0:T(8,128)} %param.13) | copy-start | bytes 772
  3.8 5.7 %copy-start.2 = (s32[6,1536]{1,0:T(8,128)S(1)}, s32[6,1536]{1,0:T(8,128)}, u32[]{:S(2)}) copy-start(s32[6,1536]{1,0:T(8,128)} %param.10) | copy-start | bytes 110596
  3.8 5.8 %copy-start.1 = (f32[2,6,768]{2,0,1:T(2,128)S(1)}, f32[2,6,768]{2,0,1:T(2,128)}, u32[]{:S(2)}) copy-start(f32[2,6,768]{2,0,1:T(2,128)} %param.8) | copy-start | bytes 110596
  5.2 6.0 %collective-permute-start.2 = (f32[2,2,3,8,1536]{4,3,2,1,0:T(8,128)S(1)}, f32[2,2,3,8,1536]{4,3,2,1,0:T(8,128)S(1)}, u32[]{:S(2)}, u32[]{:S(2)}) collective-permute-start(f32[2,2,3,8,1536]{4,3,2,1,0:T(8,128)S(1)} %get-tuple-element.32.refs_4_), channel_id=1, source_target_pairs={{0,1},{2,3},{4,5},{6,7},{8,9},{10,11},{12,13},{14,15},{1,0},{3,2},... | collective-permute-start | bytes 1769480 | tf_op jit(solution)/shard_map/ppermute | solution.py:340
  5.2 26.2 %collective-permute-start = (f32[2,2,3,8,1536]{4,3,2,1,0:T(8,128)S(1)}, f32[2,2,3,8,1536]{4,3,2,1,0:T(8,128)S(1)}, u32[]{:S(2)}, u32[]{:S(2)}) collective-permute-start(f32[2,2,3,8,1536]{4,3,2,1,0:T(8,128)S(1)} %get-tuple-element.33.refs_5_.a_out), channel_id=1, source_target_pairs={{1,2},{3,4},{5,6},{7,8},{9,10},{11,12},{13,14},{2,1},{4,3},{6,5},{... | collective-permute-start | bytes 1769480 | tf_op jit(solution)/shard_map/ppermute | solution.py:343
  9.7 1.4 %collective-permute-start.4 = (f32[6,4,1536]{2,1,0:T(4,128)S(1)}, f32[6,4,1536]{2,1,0:T(4,128)S(1)}, u32[]{:S(2)}, u32[]{:S(2)}) collective-permute-start(f32[6,4,1536]{2,1,0:T(4,128)S(1)} %pad_maximum_fusion.refs_7_.refs_8_.sea_own), channel_id=1, source_target_pairs={{0,1},{2,3},{4,5},{6,7},{8,9},{10,11},{12,13},{14,15},{1,0},{3,2},... | collective-permute-start | bytes 442376 | tf_op jit(solution)/shard_map/ppermute | solution.py:340
  17.5 33.6 %collective-permute-start.9 = (f32[2,2,3,8,1536]{4,3,2,1,0:T(8,128)S(1)}, f32[2,2,3,8,1536]{4,3,2,1,0:T(8,128)S(1)}, u32[]{:S(2)}, u32[]{:S(2)}) collective-permute-start(f32[2,2,3,8,1536]{4,3,2,1,0:T(8,128)S(1)} %get-tuple-element.24.refs_4_), channel_id=1, source_target_pairs={{0,1},{2,3},{4,5},{6,7},{8,9},{10,11},{12,13},{14,15},{1,0},{3,2},... | collective-permute-start | bytes 1769480 | tf_op jit(solution)/shard_map/ppermute | solution.py:340
  17.7 42.7 %collective-permute-start.1 = (f32[2,2,3,8,1536]{4,3,2,1,0:T(8,128)S(1)}, f32[2,2,3,8,1536]{4,3,2,1,0:T(8,128)S(1)}, u32[]{:S(2)}, u32[]{:S(2)}) collective-permute-start(f32[2,2,3,8,1536]{4,3,2,1,0:T(8,128)S(1)} %get-tuple-element.32.refs_4_), channel_id=1, source_target_pairs={{1,2},{3,4},{5,6},{7,8},{9,10},{11,12},{13,14},{2,1},{4,3},{6,5},{... | collective-permute-start | bytes 1769480 | tf_op jit(solution)/shard_map/ppermute | solution.py:343
  20.8 10.7 %collective-permute-start.5 = (f32[6,4,1536]{2,1,0:T(4,128)S(1)}, f32[6,4,1536]{2,1,0:T(4,128)S(1)}, u32[]{:S(2)}, u32[]{:S(2)}) collective-permute-start(f32[6,4,1536]{2,1,0:T(4,128)S(1)} %pad_maximum_fusion.refs_7_.refs_8_.sea_own), channel_id=1, source_target_pairs={{1,2},{3,4},{5,6},{7,8},{9,10},{11,12},{13,14},{2,1},{4,3},{6,5},{... | collective-permute-start | bytes 442376 | tf_op jit(solution)/shard_map/ppermute | solution.py:343
  36.1 4.4 %collective-permute-start.6 = (f32[6,2,1536]{2,1,0:T(2,128)S(1)}, f32[6,2,1536]{2,1,0:T(2,128)S(1)}, u32[]{:S(2)}, u32[]{:S(2)}) collective-permute-start(f32[6,2,1536]{2,1,0:T(2,128)S(1)} %get-tuple-element.22), channel_id=1, source_target_pairs={{0,16},{16,0},{1,17},{17,1},{2,18},{18,2},{3,19},{19,3},{4,20},{20... | collective-permute-start | bytes 221192 | tf_op jit(solution)/shard_map/ppermute | solution.py:347
  40.5 10.6 %collective-permute-start.7 = (f32[6,2,1536]{2,1,0:T(2,128)S(1)}, f32[6,2,1536]{2,1,0:T(2,128)S(1)}, u32[]{:S(2)}, u32[]{:S(2)}) collective-permute-start(f32[6,2,1536]{2,1,0:T(2,128)S(1)} %add.62.refs_10_.refs_11_.f_own), channel_id=1, source_target_pairs={{0,1},{2,3},{4,5},{6,7},{8,9},{10,11},{12,13},{14,15},{1,0},{3,2},... | collective-permute-start | bytes 221192 | tf_op jit(solution)/shard_map/ppermute | solution.py:340
  47.0 13.4 %collective-permute-start.8 = (f32[6,2,1536]{2,1,0:T(2,128)S(1)}, f32[6,2,1536]{2,1,0:T(2,128)S(1)}, u32[]{:S(2)}, u32[]{:S(2)}) collective-permute-start(f32[6,2,1536]{2,1,0:T(2,128)S(1)} %add.62.refs_10_.refs_11_.f_own), channel_id=1, source_target_pairs={{1,2},{3,4},{5,6},{7,8},{9,10},{11,12},{13,14},{2,1},{4,3},{6,5},{... | collective-permute-start | bytes 221192 | tf_op jit(solution)/shard_map/ppermute | solution.py:343
  71.9 4.4 %collective-permute-start.10 = (f32[6,2,1536]{2,1,0:T(2,128)S(1)}, f32[6,2,1536]{2,1,0:T(2,128)S(1)}, u32[]{:S(2)}, u32[]{:S(2)}) collective-permute-start(f32[6,2,1536]{2,1,0:T(2,128)S(1)} %get-tuple-element.31), channel_id=1, source_target_pairs={{0,16},{16,0},{1,17},{17,1},{2,18},{18,2},{3,19},{19,3},{4,20},{20... | collective-permute-start | bytes 221192 | tf_op jit(solution)/shard_map/ppermute | solution.py:347
  76.4 5.9 %collective-permute-start.12 = (f32[1,2,1536]{2,1,0:T(2,128)S(1)}, f32[1,2,1536]{2,1,0:T(2,128)S(1)}, u32[]{:S(2)}, u32[]{:S(2)}) collective-permute-start(f32[1,2,1536]{2,1,0:T(2,128)S(1)} %get-tuple-element.36), channel_id=1, source_target_pairs={{1,2},{3,4},{5,6},{7,8},{9,10},{11,12},{13,14},{2,1},{4,3},{6,5},{... | collective-permute-start | bytes 36872 | tf_op jit(solution)/shard_map/ppermute | solution.py:343
  78.6 3.7 %collective-permute-start.11 = (f32[1,2,1536]{2,1,0:T(2,128)S(1)}, f32[1,2,1536]{2,1,0:T(2,128)S(1)}, u32[]{:S(2)}, u32[]{:S(2)}) collective-permute-start(f32[1,2,1536]{2,1,0:T(2,128)S(1)} %get-tuple-element.37), channel_id=1, source_target_pairs={{0,1},{2,3},{4,5},{6,7},{8,9},{10,11},{12,13},{14,15},{1,0},{3,2},... | collective-permute-start | bytes 36872 | tf_op jit(solution)/shard_map/ppermute | solution.py:340

commit v2 on v1

--- a/solution.py
+++ b/solution.py
@@ -19,6 +19,7 @@
 VMEM = pl.BlockSpec(memory_space=pltpu.VMEM)
 SMEM = pl.BlockSpec(memory_space=pltpu.SMEM)
 LANES = 128
+QUARTERS = 4
 
 
 def place(up, row, base, count):
@@ -50,6 +51,12 @@
     def wait(self):
         for copy in self.started:
             copy.wait()
+
+
+def sea_piece(ref, row, c, t, lon):
+    per = lon // QUARTERS // LANES
+    line, part = c * QUARTERS + t // per, t % per
+    return ref[row, line : line + 1, part * LANES : (part + 1) * LANES]
 
 
 def atmos_rows(up, reals, coef, source, target, surface, first, count, edge, valid):
@@ -86,7 +93,7 @@
                     total = coef[c, m, 0] * part
                     for d in range(1, 8):
                         total += coef[c, m, d] * pltpu.roll(part, 8 - d, 0)
-                    total += relax * srf[sea, c : c + 1, t * LANES : (t + 1) * LANES]
+                    total += relax * sea_piece(srf, sea, c, t, lon)
                     if edge is not None:
                         total = total * jnp.where(row >= edge, valid, 1.0)
                     dst[c, m, there, :, t * LANES : (t + 1) * LANES] = total
@@ -99,19 +106,22 @@
     st, st_base, st_rows = state
     srf, srf_base, srf_rows = surface
     ref, base, rows = out
-    members = st.shape[1]
+    members, lon = st.shape[1], st.shape[4]
 
     def one(i, carry):
         row = first + i
         at = place(up, row, st_base, st_rows)
         sea = place(up, row, srf_base, srf_rows)
         to = place(up, row, base, rows)
+        per = lon // QUARTERS // LANES
         for c in range(2):
-            s = srf[sea, c : c + 1, :]
-            flux = jnp.zeros_like(s)
-            for m in range(members):
-                flux += reals[members + c * members + m] * (st[c, m, at, 0:1, :] - s)
-            ref[to, c : c + 1, :] = flux * (1.0 / ensemble)
+            for t in range(lon // LANES):
+                s = sea_piece(srf, sea, c, t, lon)
+                flux = jnp.zeros_like(s)
+                for m in range(members):
+                    flux += reals[members + c * members + m] * (st[c, m, at, 0:1, t * LANES : (t + 1) * LANES] - s)
+                line, part = c * QUARTERS + t // per, t % per
+                ref[to, line : line + 1, part * LANES : (part + 1) * LANES] = flux * (1.0 / ensemble)
         return carry
 
     lax.fori_loop(0, count, one, 0)
@@ -122,27 +132,29 @@
     fixed, fixed_base, fixed_rows = sea
     frc, frc_base, frc_rows = forcing
     dst, dst_base, dst_rows = target
-    lon = src.shape[2]
-
-    def one(i, carry):
+    lines, lon = src.shape[1:]
+    line = lax.broadcasted_iota(jnp.int32, (lines, lon), 0)
+    lane = lax.broadcasted_iota(jnp.int32, (lines, lon), 1)
+    quarter = line % QUARTERS
+
+    for i in range(count):
         row = first + i
         here = place(up, row, src_base, src_rows)
         cell = place(up, row, fixed_base, fixed_rows)
         force = place(up, row, frc_base, frc_rows)
         to = place(up, row, dst_base, dst_rows)
-        mask = fixed[cell, 3:4, :]
-        for c in range(2):
-            centre = src[here, c : c + 1, :]
-            laplace = (
-                (pltpu.roll(centre, lon - 1, 1) + pltpu.roll(centre, 1, 1))
-                + (src[here - 1, c : c + 1, :] + src[here + 1, c : c + 1, :])
-                - 4.0 * centre
-            )
-            rate = OCEAN_DIFFUSION if c == 0 else fixed[cell, 2:3, :]
-            dst[to, c : c + 1, :] = centre + mask * (OCEAN_GAIN * frc[force, c : c + 1, :] + rate * laplace)
-        return carry
-
-    lax.fori_loop(0, count, one, 0)
+        both = fixed[cell]
+        turned = pltpu.roll(both, QUARTERS, 0)
+        mask = jnp.where(line < QUARTERS, turned, both)
+        rate = jnp.where(line < QUARTERS, OCEAN_DIFFUSION, turned)
+        centre = src[here]
+        eastern, western = pltpu.roll(centre, lon - 1, 1), pltpu.roll(centre, 1, 1)
+        after = jnp.where(quarter == QUARTERS - 1, pltpu.roll(eastern, QUARTERS - 1, 0), pltpu.roll(eastern, lines - 1, 0))
+        before = jnp.where(quarter == 0, pltpu.roll(western, lines - QUARTERS + 1, 0), pltpu.roll(western, 1, 0))
+        eastern = jnp.where(lane == lon - 1, after, eastern)
+        western = jnp.where(lane == 0, before, western)
+        laplace = (eastern + western) + (src[here - 1] + src[here + 1]) - 4.0 * centre
+        dst[to] = centre + mask * (OCEAN_GAIN * frc[force] + rate * laplace)
 
 
 def load_three(up, group, target, band, low, own, high):
@@ -180,14 +192,14 @@
         force, middle, surf = refs
         load_three(up, loads, force, band, f_low, f_own, f_high)
     loads.wait()
-    fixed = (sea, -band, whole)
+    start, fixed = (sea.at[:, 0], -band, whole), (sea.at[:, 1], -band, whole)
     if coupled:
         forcing, half = (force, -band, whole), (middle, -band, whole)
-        ocean_rows(up, fixed, fixed, forcing, half, -H, 2 * H + 3)
+        ocean_rows(up, fixed, start, forcing, half, -H, 2 * H + 3)
         surface = (surf, -band, whole)
         ocean_rows(up, fixed, half, forcing, surface, -H + 1, 2 * H + 1)
     else:
-        surface = fixed
+        surface = start
     step0, step1, step2 = (win, -H, size), (lev1, 1 - H, 7), (lev2, 2 - H, 5)
     step3 = (done, 0, H)
     atmos_rows(up, reals, coef, step0, step1, surface, 1 - H, 7, None, None)
@@ -221,7 +233,7 @@
     load_three(up, loads, sea, band, sea_low, sea_own, sea_high)
     loads.start(flux_in, flux.at[pl.ds(chunk(up, 0, H, 0, band), H)])
     loads.wait()
-    surface = (sea, -band, 3 * band)
+    surface = (sea.at[:, 0], -band, 3 * band)
     tile(up, reals, coef, win, lev1, lev2, (done, 3, 3), 5, surface, band, valid)
     stores = pool.copies()
     stores.start(lev1.at[:, :, pl.ds(chunk(up, 6, 2, 3, 5), 2)], next1)
@@ -251,11 +263,12 @@
     loads.wait()
     stores = pool.copies()
     stores.start(b_in, result.at[:, :, pl.ds(chunk(up, 0, H, 0, band), H)])
-    fixed, forcing, half = (sea, -band, whole), (force, -band, whole), (middle, -band, whole)
+    start, fixed = (sea.at[:, 0], -band, whole), (sea.at[:, 1], -band, whole)
+    forcing, half = (force, -band, whole), (middle, -band, whole)
     surface = (surf, -band, whole)
-    ocean_rows(up, fixed, fixed, forcing, half, -3, 12)
+    ocean_rows(up, fixed, start, forcing, half, -3, 12)
     ocean_rows(up, fixed, half, forcing, surface, -2, 10)
-    tile(up, reals, coef, win, lev1, lev2, (win_b, 4, 5), 8, fixed, band, valid)
+    tile(up, reals, coef, win, lev1, lev2, (win_b, 4, 5), 8, start, band, valid)
     tile(up, reals, coef, win_b, lev1_b, lev2_b, (done, 3, 3), 5, surface, band, valid)
     stores.start(done, result.at[:, :, pl.ds(chunk(up, 3, H, 0, band), H)])
     stores.start(surf, surface_out)
@@ -276,14 +289,19 @@
     loads.start(f_own, force.at[pl.ds(1, band)])
     loads.start(f_high, force.at[pl.ds(chunk(up, band, 1, -1, band + 2), 1)])
     loads.wait()
-    fixed, ocean = (sea, -band, whole), (surf, -band, whole)
+    fixed, ocean = (sea.at[:, 1], -band, whole), (surf, -band, whole)
     forcing, half = (force, -1, band + 2), (middle, -1, band + 2)
     ocean_rows(up, fixed, ocean, forcing, half, -1, band + 2)
     ocean_rows(up, fixed, half, forcing, (final, 0, band), 0, band)
     if tile_width is None:
         out[...] = final[...]
     else:
-        out[...] = final[:, :, pl.ds(pl.multiple_of(ints[1] * tile_width, LANES), tile_width)]
+        lon = final.shape[2]
+        for row in range(band):
+            for c in range(2):
+                for part in range(tile_width // lon):
+                    line = c * QUARTERS + ints[1] * (tile_width // lon) + part
+                    out[row, c : c + 1, part * lon : (part + 1) * lon] = final[row, pl.ds(line, 1), :]
 
 
 def call(kernel, name, outs, scratch, args, copies, flops=0):
@@ -356,14 +374,20 @@
 
     state = jnp.transpose(atmosphere, (0, 1, 3, 2, 4))
     a_out = lax.dynamic_slice_in_dim(state, up * H, H, 2)
-    a_high = to_far(a_out)
     a_in = lax.dynamic_slice_in_dim(state, (1 - up) * H, H, 2)
     a_low = to_near(a_in)
 
+    ocean_state, viscosity, a_out = lax.optimization_barrier((ocean_state, viscosity, a_out))
     tile_fields = jnp.concatenate([jnp.transpose(ocean_state, (1, 0, 2)), viscosity[:, None]], axis=1)
-    sea_own = jnp.concatenate([full_rows(tile_fields), sea_mask.astype(jnp.float32)[:, None]], axis=1)
+    a_high = to_far(a_out)
+    packed = (band, 1, fields * QUARTERS, lon // QUARTERS)
+    sea_tile = full_rows(tile_fields)
+    masked = jnp.concatenate([sea_tile[:, 2:], sea_mask.astype(jnp.float32)[:, None]], axis=1)
+    sea_own = jnp.concatenate([sea_tile[:, :2].reshape(packed), masked.reshape(packed)], axis=1)
     sea_low, sea_high = to_near(sea_own), to_far(sea_own)
 
+    sea_high, far_rows = lax.optimization_barrier((sea_high, a_in))
+    a_far = to_far(far_rows)
     diffusivity, exchange = lookup(parameter_index, parameter_table)
     coef = mixing(level_mix, exchange)
     valid = jnp.where(up == 1, position < bands - 1, position > 0).astype(jnp.float32)
@@ -372,6 +396,11 @@
     common = [("smem", ints), ("smem", reals), ("vmem", coef)]
     seas = [("any", sea_low), ("any", sea_own), ("any", sea_high)]
 
+    def band_shape(n):
+        return (n, fields * QUARTERS, lon // QUARTERS)
+
+    sea_shape = (3 * band, 2, fields * QUARTERS, lon // QUARTERS)
+
     def rows(n):
         return (fields, members, n, levels, lon)
 
@@ -379,21 +408,20 @@
     unit = members * fields * levels * lon * 30
 
     def inner(coupled, low, inside, outside, sea3, force3, name):
-        outs = [("vmem", rows(H)), ("any", rows(2)), ("any", rows(2)), ("vmem", (H, fields, lon))]
-        scratch = [rows(3 * H), rows(7), rows(5), (3 * band, 4, lon)]
+        outs = [("vmem", rows(H)), ("any", rows(2)), ("any", rows(2)), ("vmem", band_shape(H))]
+        scratch = [rows(3 * H), rows(7), rows(5), sea_shape]
         if coupled:
-            scratch += [(3 * band, 2, lon)] * 3
-            outs += [("any", (3 * band, 2, lon))]
+            scratch += [band_shape(3 * band)] * 3
+            outs += [("any", band_shape(3 * band))]
         args = common + [("any", low), ("any", inside), ("any", outside)] + sea3 + force3
         return call(functools.partial(inner_kernel, cfg, coupled), name, outs, scratch, args, 16, 15 * unit)
 
     b_in, carry1, carry2, flux = inner(False, a_low, a_in, a_out, seas[:2] + [("any", sea_own)], [], "inner_first")
-    a_far = to_far(a_in)
     b_low = to_near(b_in)
     b_out, carry1, carry2, flux = call(
         functools.partial(outer_kernel, cfg), "outer_first",
-        [("vmem", rows(H)), ("any", rows(2)), ("any", rows(2)), ("vmem", (band, fields, lon))],
-        [rows(5), rows(5), rows(5), (3 * band, 4, lon)],
+        [("vmem", rows(H)), ("any", rows(2)), ("any", rows(2)), ("vmem", band_shape(band))],
+        [rows(5), rows(5), rows(5), sea_shape],
         common + [("any", a_out), ("any", a_high), ("any", carry1), ("any", carry2), ("any", flux)] + seas, 16, 9 * unit)
     f_own = total(flux)
     f_low, f_high = to_near(f_own), to_far(f_own)
@@ -402,22 +430,22 @@
         [("any", f_low), ("any", f_own), ("any", f_own)], "inner_second")
     result, flux, surface = call(
         functools.partial(last_kernel, cfg), "outer_second",
-        [("any", rows(band)), ("vmem", (band, fields, lon)), ("any", (3 * band, 2, lon))],
-        [rows(5)] * 6 + [rows(H), (3 * band, 4, lon)] + [(3 * band, 2, lon)] * 3,
+        [("any", rows(band)), ("vmem", band_shape(band)), ("any", band_shape(3 * band))],
+        [rows(5)] * 6 + [rows(H), sea_shape] + [band_shape(3 * band)] * 3,
         common + [("any", a_high), ("any", a_far), ("any", carry1), ("any", carry2)] + seas
         + [("any", f_low), ("any", f_own), ("any", f_high), ("any", b_out), ("any", c_in), ("any", b_carry1), ("any", b_carry2), ("any", flux)],
         24, 18 * unit)
     g_own = total(flux)
     g_low = to_near(lax.dynamic_slice_in_dim(g_own, (1 - up) * (band - 1), 1, 0))
     g_high = to_far(lax.dynamic_slice_in_dim(g_own, up * (band - 1), 1, 0))
-    inside_kernel = width % LANES == 0
+    inside_kernel = width % (lon // QUARTERS) == 0
     (ocean,) = call(
         functools.partial(ocean_kernel, (band, H, width if inside_kernel else None)), "ocean_last",
-        [("vmem", (band, fields, width if inside_kernel else lon))],
-        [(3 * band, 4, lon), (3 * band, 2, lon), (band + 2, 2, lon), (band + 2, 2, lon), (band, 2, lon)],
+        [("vmem", (band, fields, width) if inside_kernel else band_shape(band))],
+        [sea_shape, band_shape(3 * band), band_shape(band + 2), band_shape(band + 2), band_shape(band)],
         [("smem", ints), ("any", surface)] + seas + [("any", g_low), ("any", g_own), ("any", g_high)], 8)
     if not inside_kernel:
-        ocean = lax.dynamic_slice_in_dim(ocean, side * width, width, 2)
+        ocean = lax.dynamic_slice_in_dim(ocean.reshape(band, fields, lon), side * width, width, 2)
     return (jnp.transpose(result, (0, 1, 3, 2, 4)), jnp.transpose(ocean, (1, 0, 2)))
 
 

time: 86.7 us -> 68.5 us (0.79)
  waiting for transfers between devices: 18.9 us -> 10.5 us
  Pallas kernels: 35.6 us -> 29.8 us
  starting transfers between devices: 26.5 us -> 23.9 us
  other arithmetic: 1.68 us -> 0.74 us
    ppermute x5, waiting for transfers between devices: 10.3 us -> 2.87 us  [to_far(): return lax.ppermute(x, 'lat', far)]
    pallas_call x5, Pallas kernels: 35.6 us -> 29.8 us  [call(): pl.pallas_call(kernel, name=name, out_shape=[jax.ShapeDtypeStruct(shape,...]
    ppermute x5, starting transfers between devices: 16.2 us -> 14.3 us  [to_far(): return lax.ppermute(x, 'lat', far)]
    ppermute x5, waiting for transfers between devices: 0.91 us -> 0.01 us  [to_near(): return lax.ppermute(x, 'lat', near)]
  transfers between devices with their start and end apart: 13 -> 13, of which waited for: 5 -> 3; matrix products, arithmetic and copies ran while one was open for 3% -> 2% of each run, Pallas kernels for 23% -> 27%
where the time goes in v2:
time: 68.5 us; the launch traced here: 68.2 us
  Pallas kernels  29.8 us (44%)
  starting transfers between devices  23.9 us (35%)
  waiting for transfers between devices  10.5 us (15%)
  local copies, waits for them, and re-layouts  2.05 us (3%)
  between operations  0.98 us (1%)
  other arithmetic  0.74 us (1%)
    pallas_call x5, Pallas kernels, call(): pl.pallas_call(kernel, name=name, out_shape=[jax.ShapeDtypeStruct(shape,...  29.8 us
    ppermute x5, starting transfers between devices, to_far(): return lax.ppermute(x, 'lat', far)  14.3 us
    ppermute x2, waiting for transfers between devices, total(): return x + lax.ppermute(x, 'member', other)  7.64 us
    ppermute x5, starting transfers between devices, to_near(): return lax.ppermute(x, 'lat', near)  6.83 us
    ppermute x5, waiting for transfers between devices, to_far(): return lax.ppermute(x, 'lat', far)  2.87 us
    ppermute x1, starting transfers between devices, full_rows(): y = lax.ppermute(x, 'member', other)  1.56 us
    dynamic_slice x1, local copies, waits for them, and re-layouts, body(): a_in = lax.dynamic_slice_in_dim(state, (1 - up) * H, H, 2)  1.38 us
  transfers between devices with their start and end apart: 13, of which 3 were waited for; matrix products, arithmetic and copies ran while one was open for 2% of the time, Pallas kernels for 27%

profile of v2, /device:TPU:8, one launch (start us, length us, event | category | flops | bytes accessed | tf_op | source)
XLA Modules:
  0.0 68.2 jit_solution(1152239817115500709)
XLA Ops:
  0.7 1.4 %dynamic-slice_bitcast_fusion = (f32[2,2,3,8,1536]{4,3,2,1,0:T(8,128)S(1)}, f32[2,2,3,8,1536]{4,3,2,1,0:T(8,128)S(1)}) fusion(f32[2,2,8,6,1536]{4,2,3,1,0:T(8,128)} %param.7, s32[]{:T(128)S(6)} %select_n.62, s32[]{:T(128)S(6)} %select_n.58), kind=kLoop, calls=%fused_computation | loop fusion | bytes 2359304 | tf_op jit(solution)/shard_map/dynamic_slice | solution.py:377
  2.2 1.6 %collective-permute-start.1 = (f32[6,3,768]{2,0,1:T(8,128)S(1)}, f32[6,3,768]{2,0,1:T(8,128)S(1)}, u32[]{:S(2)}, u32[]{:S(2)}) collective-permute-start(f32[6,3,768]{2,0,1:T(8,128)S(1)} %pad_maximum_fusion.1), channel_id=1, source_target_pairs={{0,16},{16,0},{1,17},{17,1},{2,18},{18,2},{3,19},{19,3},{4,20},{20... | collective-permute-start | bytes 165896 | tf_op jit(solution)/shard_map/ppermute | solution.py:370
  3.7 2.5 %collective-permute-start = (f32[2,2,3,8,1536]{4,3,2,1,0:T(8,128)S(1)}, f32[2,2,3,8,1536]{4,3,2,1,0:T(8,128)S(1)}, u32[]{:S(2)}, u32[]{:S(2)}) collective-permute-start(f32[2,2,3,8,1536]{4,3,2,1,0:T(8,128)S(1)} %get-tuple-element.22.refs_5_.a_out), channel_id=1, source_target_pairs={{1,2},{3,4},{5,6},{7,8},{9,10},{11,12},{13,14},{2,1},{4,3},{6,5},{... | collective-permute-start | bytes 1769480 | tf_op jit(solution)/shard_map/ppermute | solution.py:361
  6.2 1.1 %collective-permute-start.4 = (f32[2,2,3,8,1536]{4,3,2,1,0:T(8,128)S(1)}, f32[2,2,3,8,1536]{4,3,2,1,0:T(8,128)S(1)}, u32[]{:S(2)}, u32[]{:S(2)}) collective-permute-start(f32[2,2,3,8,1536]{4,3,2,1,0:T(8,128)S(1)} %get-tuple-element.25.refs_4_), channel_id=1, source_target_pairs={{0,1},{2,3},{4,5},{6,7},{8,9},{10,11},{12,13},{14,15},{1,0},{3,2},... | collective-permute-start | bytes 1769480 | tf_op jit(solution)/shard_map/ppermute | solution.py:358
  7.3 0.2 fusion.6
  7.9 0.2 select_reduce_fusion
  8.0 0.1 multiply_reduce_fusion
  8.6 3.4 %collective-permute-start.2 = (f32[6,2,8,384]{3,2,1,0:T(8,128)S(1)}, f32[6,2,8,384]{3,2,1,0:T(8,128)S(1)}, u32[]{:S(2)}, u32[]{:S(2)}) collective-permute-start(f32[6,2,8,384]{3,2,1,0:T(8,128)S(1)} %constant_dynamic-update-slice_fusion.refs_7_.refs_8_.sea_own), channel_id=1, source_target_pairs={{1,2},{3,4},{5,6},{7,8},{9,10},{11,12},{13,14},{2,1},{4,3},{6,5},{... | collective-permute-start | bytes 442376 | tf_op jit(solution)/shard_map/ppermute | solution.py:361
  12.5 6.3 %inner_first.1 = (f32[2,2,3,8,1536]{4,3,2,1,0:T(8,128)S(1)}, f32[2,2,2,8,1536]{4,3,2,1,0:T(8,128)S(1)}, f32[2,2,2,8,1536]{4,3,2,1,0:T(8,128)S(1)}, f32[3,8,384]{2,1,0:T(8,128)S(1)}) custom-call(s32[2]{0:T(128)S(1)} %pad_add_fusion.refs_0_.ints, f32[7]{0:T(128)S(1)} %pad_maximum_fusion.2.refs_1_.reals, ...), custom_call_target="tpu_custom_call" | custom-call | flops 22118400 | bytes 4194304 | tf_op jit(solution)/shard_map/inner_first/pallas_call | solution.py:309
  18.7 0.2 collective-permute-start.9
  18.9 2.9 %collective-permute-start.3 = (f32[2,2,3,8,1536]{4,3,2,1,0:T(8,128)S(1)}, f32[2,2,3,8,1536]{4,3,2,1,0:T(8,128)S(1)}, u32[]{:S(2)}, u32[]{:S(2)}) collective-permute-start(f32[2,2,3,8,1536]{4,3,2,1,0:T(8,128)S(1)} %get-tuple-element.25.refs_4_), channel_id=1, source_target_pairs={{1,2},{3,4},{5,6},{7,8},{9,10},{11,12},{13,14},{2,1},{4,3},{6,5},{... | collective-permute-start | bytes 1769480 | tf_op jit(solution)/shard_map/ppermute | solution.py:361
  21.9 4.6 %outer_first.1 = (f32[2,2,3,8,1536]{4,3,2,1,0:T(8,128)S(1)}, f32[2,2,2,8,1536]{4,3,2,1,0:T(8,128)S(1)}, f32[2,2,2,8,1536]{4,3,2,1,0:T(8,128)S(1)}, f32[6,8,384]{2,1,0:T(8,128)S(1)}) custom-call(s32[2]{0:T(128)S(1)} %pad_add_fusion.refs_0_.ints, f32[7]{0:T(128)S(1)} %pad_maximum_fusion.2.refs_1_.reals, ...), custom_call_target="tpu_custom_call" | custom-call | flops 13271040 | bytes 4194304 | tf_op jit(solution)/shard_map/outer_first/pallas_call | solution.py:309
  26.5 0.6 collective-permute-start.6
  27.1 3.8 %collective-permute-done.6 = f32[6,8,384]{2,1,0:T(8,128)S(1)} collective-permute-done((f32[6,8,384]{2,1,0:T(8,128)S(1)}, f32[6,8,384]{2,1,0:T(8,128)S(1)}, u32[]{:S(2)}, u32[]{:S(2)}) %collective-permute-start.6) | collective-permute-done | bytes 73760 | tf_op jit(solution)/shard_map/ppermute | solution.py:365
  30.9 5.0 %collective-permute-start.7 = (f32[6,8,384]{2,1,0:T(8,128)S(1)}, f32[6,8,384]{2,1,0:T(8,128)S(1)}, u32[]{:S(2)}, u32[]{:S(2)}) collective-permute-start(f32[6,8,384]{2,1,0:T(8,128)S(1)} %add.62.refs_10_.refs_11_.f_own), channel_id=1, source_target_pairs={{0,1},{2,3},{4,5},{6,7},{8,9},{10,11},{12,13},{14,15},{1,0},{3,2},... | collective-permute-start | bytes 221192 | tf_op jit(solution)/shard_map/ppermute | solution.py:358
  35.9 2.9 %collective-permute-start.8 = (f32[6,8,384]{2,1,0:T(8,128)S(1)}, f32[6,8,384]{2,1,0:T(8,128)S(1)}, u32[]{:S(2)}, u32[]{:S(2)}) collective-permute-start(f32[6,8,384]{2,1,0:T(8,128)S(1)} %add.62.refs_10_.refs_11_.f_own), channel_id=1, source_target_pairs={{1,2},{3,4},{5,6},{7,8},{9,10},{11,12},{13,14},{2,1},{4,3},{6,5},{... | collective-permute-start | bytes 221192 | tf_op jit(solution)/shard_map/ppermute | solution.py:361
  38.9 7.5 %inner_second.1 = (f32[2,2,3,8,1536]{4,3,2,1,0:T(8,128)S(1)}, f32[2,2,2,8,1536]{4,3,2,1,0:T(8,128)S(1)}, f32[2,2,2,8,1536]{4,3,2,1,0:T(8,128)S(1)}, f32[3,8,384]{2,1,0:T(8,128)S(1)}, f32[18,8,384]{2,1,0:T(8,128)}) custom-call(s32[2]{0:T(128)S(1)} %pad_add_fusion.refs_0_.ints, f32[7]{0:T(128)S(1)} %pad_maximum_fusion.2.refs_1_.reals, ...), custom_call_target="tpu_custom_call" | custom-call | flops 22118400 | bytes 4194304 | tf_op jit(solution)/shard_map/inner_second/pallas_call | solution.py:309
  46.4 9.0 %outer_second.1 = (f32[2,2,6,8,1536]{4,3,2,1,0:T(8,128)}, f32[6,8,384]{2,1,0:T(8,128)S(1)}, f32[18,8,384]{2,1,0:T(8,128)S(1)}) custom-call(s32[2]{0:T(128)S(1)} %pad_add_fusion.refs_0_.ints, f32[7]{0:T(128)S(1)} %pad_maximum_fusion.2.refs_1_.reals, f32[2,2,8,8,128]{4,3,2,1,0:T(8,128)S(1)} %broadcast_in_dim.48.refs_2_.coef, ...), custom_call_target="tpu_custom_call" | custom-call | flops 26542080 | bytes 4194304 | tf_op jit(solution)/shard_map/outer_second/pallas_call | solution.py:309
  55.4 0.6 collective-permute-start.10
  56.0 3.8 %collective-permute-done.10 = f32[6,8,384]{2,1,0:T(8,128)S(1)} collective-permute-done((f32[6,8,384]{2,1,0:T(8,128)S(1)}, f32[6,8,384]{2,1,0:T(8,128)S(1)}, u32[]{:S(2)}, u32[]{:S(2)}) %collective-permute-start.10) | collective-permute-done | bytes 73760 | tf_op jit(solution)/shard_map/ppermute | solution.py:365
  59.8 2.6 %collective-permute-start.12 = (f32[1,8,384]{2,1,0:T(8,128)S(1)}, f32[1,8,384]{2,1,0:T(8,128)S(1)}, u32[]{:S(2)}, u32[]{:S(2)}) collective-permute-start(f32[1,8,384]{2,1,0:T(8,128)S(1)} %get-tuple-element.48), channel_id=1, source_target_pairs={{1,2},{3,4},{5,6},{7,8},{9,10},{11,12},{13,14},{2,1},{4,3},{6,5},{... | collective-permute-start | bytes 36872 | tf_op jit(solution)/shard_map/ppermute | solution.py:361
  62.4 0.4 collective-permute-start.11
  62.9 2.9 %collective-permute-done.12.f_high = f32[1,8,384]{2,1,0:T(8,128)S(1)} collective-permute-done((f32[1,8,384]{2,1,0:T(8,128)S(1)}, f32[1,8,384]{2,1,0:T(8,128)S(1)}, u32[]{:S(2)}, u32[]{:S(2)}) %collective-permute-start.12) | collective-permute-done | bytes 12320 | tf_op jit(solution)/shard_map/ppermute | solution.py:361
  65.7 2.5 %ocean_last.1 = f32[6,2,768]{2,1,0:T(2,128)} custom-call(s32[2]{0:T(128)S(1)} %pad_add_fusion.refs_0_.ints, f32[18,8,384]{2,1,0:T(8,128)S(1)} %get-tuple-element.40.surface_in, f32[6,2,8,384]{3,2,1,0:T(8,128)S(1)} %collective-permute-done.5.refs_6_.sea_low, f32[6,2,8,384]{3,2,1,0:T(8,128)S(1)} %constant_dynamic-update-slice_fusion.refs_7_.refs_8_.sea_own, ...), custom_call_target="tpu_custom_call" | custom-call | bytes 4194304 | tf_op jit(solution)/shard_map/ocean_last/pallas_call | solution.py:309
  (50 shorter events, 1.3 us)
Async XLA Ops:
  0.6 6.7 %copy-start = (f32[32,3]{0,1:T(4,128)S(1)}, f32[32,3]{0,1:T(4,128)}, u32[]{:S(2)}) copy-start(f32[32,3]{0,1:T(4,128)} %param.12) | copy-start | bytes 1156
  0.7 1.4 %copy-start.3 = (f32[2,6,768]{2,0,1:T(2,128)S(1)}, f32[2,6,768]{2,0,1:T(2,128)}, u32[]{:S(2)}) copy-start(f32[2,6,768]{2,0,1:T(2,128)} %param.8) | copy-start | bytes 110596
  0.7 1.5 %copy-start.1 = (f32[6,768]{1,0:T(8,128)S(1)}, f32[6,768]{1,0:T(8,128)}, u32[]{:S(2)}) copy-start(f32[6,768]{1,0:T(8,128)} %param.9) | copy-start | bytes 55300
  0.7 6.6 %copy-start.5 = (s32[2]{0:T(128)S(1)}, s32[2]{0:T(128)}, u32[]{:S(2)}) copy-start(s32[2]{0:T(128)} %param.11) | copy-start | bytes 28
  0.7 7.1 %copy-start.4 = (f32[8,8]{1,0:T(8,128)S(1)}, f32[8,8]{1,0:T(8,128)}, u32[]{:S(2)}) copy-start(f32[8,8]{1,0:T(8,128)} %param.13) | copy-start | bytes 772
  0.7 7.1 %copy-start.2 = (s32[6,1536]{1,0:T(8,128)S(1)}, s32[6,1536]{1,0:T(8,128)}, u32[]{:S(2)}) copy-start(s32[6,1536]{1,0:T(8,128)} %param.10) | copy-start | bytes 110596
  2.2 6.0 %collective-permute-start.1 = (f32[6,3,768]{2,0,1:T(8,128)S(1)}, f32[6,3,768]{2,0,1:T(8,128)S(1)}, u32[]{:S(2)}, u32[]{:S(2)}) collective-permute-start(f32[6,3,768]{2,0,1:T(8,128)S(1)} %pad_maximum_fusion.1), channel_id=1, source_target_pairs={{0,16},{16,0},{1,17},{17,1},{2,18},{18,2},{3,19},{19,3},{4,20},{20... | collective-permute-start | bytes 165896 | tf_op jit(solution)/shard_map/ppermute | solution.py:370
  3.7 18.2 %collective-permute-start = (f32[2,2,3,8,1536]{4,3,2,1,0:T(8,128)S(1)}, f32[2,2,3,8,1536]{4,3,2,1,0:T(8,128)S(1)}, u32[]{:S(2)}, u32[]{:S(2)}) collective-permute-start(f32[2,2,3,8,1536]{4,3,2,1,0:T(8,128)S(1)} %get-tuple-element.22.refs_5_.a_out), channel_id=1, source_target_pairs={{1,2},{3,4},{5,6},{7,8},{9,10},{11,12},{13,14},{2,1},{4,3},{6,5},{... | collective-permute-start | bytes 1769480 | tf_op jit(solution)/shard_map/ppermute | solution.py:361
  6.2 6.2 %collective-permute-start.4 = (f32[2,2,3,8,1536]{4,3,2,1,0:T(8,128)S(1)}, f32[2,2,3,8,1536]{4,3,2,1,0:T(8,128)S(1)}, u32[]{:S(2)}, u32[]{:S(2)}) collective-permute-start(f32[2,2,3,8,1536]{4,3,2,1,0:T(8,128)S(1)} %get-tuple-element.25.refs_4_), channel_id=1, source_target_pairs={{0,1},{2,3},{4,5},{6,7},{8,9},{10,11},{12,13},{14,15},{1,0},{3,2},... | collective-permute-start | bytes 1769480 | tf_op jit(solution)/shard_map/ppermute | solution.py:358
  8.5 3.8 %collective-permute-start.5 = (f32[6,2,8,384]{3,2,1,0:T(8,128)S(1)}, f32[6,2,8,384]{3,2,1,0:T(8,128)S(1)}, u32[]{:S(2)}, u32[]{:S(2)}) collective-permute-start(f32[6,2,8,384]{3,2,1,0:T(8,128)S(1)} %constant_dynamic-update-slice_fusion.refs_7_.refs_8_.sea_own), channel_id=1, source_target_pairs={{0,1},{2,3},{4,5},{6,7},{8,9},{10,11},{12,13},{14,15},{1,0},{3,2},... | collective-permute-start | bytes 442376 | tf_op jit(solution)/shard_map/ppermute | solution.py:358
  8.6 10.3 %collective-permute-start.2 = (f32[6,2,8,384]{3,2,1,0:T(8,128)S(1)}, f32[6,2,8,384]{3,2,1,0:T(8,128)S(1)}, u32[]{:S(2)}, u32[]{:S(2)}) collective-permute-start(f32[6,2,8,384]{3,2,1,0:T(8,128)S(1)} %constant_dynamic-update-slice_fusion.refs_7_.refs_8_.sea_own), channel_id=1, source_target_pairs={{1,2},{3,4},{5,6},{7,8},{9,10},{11,12},{13,14},{2,1},{4,3},{6,5},{... | collective-permute-start | bytes 442376 | tf_op jit(solution)/shard_map/ppermute | solution.py:361
  18.7 20.1 %collective-permute-start.9 = (f32[2,2,3,8,1536]{4,3,2,1,0:T(8,128)S(1)}, f32[2,2,3,8,1536]{4,3,2,1,0:T(8,128)S(1)}, u32[]{:S(2)}, u32[]{:S(2)}) collective-permute-start(f32[2,2,3,8,1536]{4,3,2,1,0:T(8,128)S(1)} %get-tuple-element.34.refs_4_), channel_id=1, source_target_pairs={{0,1},{2,3},{4,5},{6,7},{8,9},{10,11},{12,13},{14,15},{1,0},{3,2},... | collective-permute-start | bytes 1769480 | tf_op jit(solution)/shard_map/ppermute | solution.py:358
  18.9 27.4 %collective-permute-start.3 = (f32[2,2,3,8,1536]{4,3,2,1,0:T(8,128)S(1)}, f32[2,2,3,8,1536]{4,3,2,1,0:T(8,128)S(1)}, u32[]{:S(2)}, u32[]{:S(2)}) collective-permute-start(f32[2,2,3,8,1536]{4,3,2,1,0:T(8,128)S(1)} %get-tuple-element.25.refs_4_), channel_id=1, source_target_pairs={{1,2},{3,4},{5,6},{7,8},{9,10},{11,12},{13,14},{2,1},{4,3},{6,5},{... | collective-permute-start | bytes 1769480 | tf_op jit(solution)/shard_map/ppermute | solution.py:361
  26.5 4.4 %collective-permute-start.6 = (f32[6,8,384]{2,1,0:T(8,128)S(1)}, f32[6,8,384]{2,1,0:T(8,128)S(1)}, u32[]{:S(2)}, u32[]{:S(2)}) collective-permute-start(f32[6,8,384]{2,1,0:T(8,128)S(1)} %get-tuple-element.32), channel_id=1, source_target_pairs={{0,16},{16,0},{1,17},{17,1},{2,18},{18,2},{3,19},{19,3},{4,20},{20... | collective-permute-start | bytes 221192 | tf_op jit(solution)/shard_map/ppermute | solution.py:365
  30.9 7.9 %collective-permute-start.7 = (f32[6,8,384]{2,1,0:T(8,128)S(1)}, f32[6,8,384]{2,1,0:T(8,128)S(1)}, u32[]{:S(2)}, u32[]{:S(2)}) collective-permute-start(f32[6,8,384]{2,1,0:T(8,128)S(1)} %add.62.refs_10_.refs_11_.f_own), channel_id=1, source_target_pairs={{0,1},{2,3},{4,5},{6,7},{8,9},{10,11},{12,13},{14,15},{1,0},{3,2},... | collective-permute-start | bytes 221192 | tf_op jit(solution)/shard_map/ppermute | solution.py:358
  35.9 10.5 %collective-permute-start.8 = (f32[6,8,384]{2,1,0:T(8,128)S(1)}, f32[6,8,384]{2,1,0:T(8,128)S(1)}, u32[]{:S(2)}, u32[]{:S(2)}) collective-permute-start(f32[6,8,384]{2,1,0:T(8,128)S(1)} %add.62.refs_10_.refs_11_.f_own), channel_id=1, source_target_pairs={{1,2},{3,4},{5,6},{7,8},{9,10},{11,12},{13,14},{2,1},{4,3},{6,5},{... | collective-permute-start | bytes 221192 | tf_op jit(solution)/shard_map/ppermute | solution.py:361
  55.4 4.4 %collective-permute-start.10 = (f32[6,8,384]{2,1,0:T(8,128)S(1)}, f32[6,8,384]{2,1,0:T(8,128)S(1)}, u32[]{:S(2)}, u32[]{:S(2)}) collective-permute-start(f32[6,8,384]{2,1,0:T(8,128)S(1)} %get-tuple-element.41), channel_id=1, source_target_pairs={{0,16},{16,0},{1,17},{17,1},{2,18},{18,2},{3,19},{19,3},{4,20},{20... | collective-permute-start | bytes 221192 | tf_op jit(solution)/shard_map/ppermute | solution.py:365
  59.8 5.9 %collective-permute-start.12 = (f32[1,8,384]{2,1,0:T(8,128)S(1)}, f32[1,8,384]{2,1,0:T(8,128)S(1)}, u32[]{:S(2)}, u32[]{:S(2)}) collective-permute-start(f32[1,8,384]{2,1,0:T(8,128)S(1)} %get-tuple-element.48), channel_id=1, source_target_pairs={{1,2},{3,4},{5,6},{7,8},{9,10},{11,12},{13,14},{2,1},{4,3},{6,5},{... | collective-permute-start | bytes 36872 | tf_op jit(solution)/shard_map/ppermute | solution.py:361
  62.4 3.3 %collective-permute-start.11 = (f32[1,8,384]{2,1,0:T(8,128)S(1)}, f32[1,8,384]{2,1,0:T(8,128)S(1)}, u32[]{:S(2)}, u32[]{:S(2)}) collective-permute-start(f32[1,8,384]{2,1,0:T(8,128)S(1)} %get-tuple-element.49), channel_id=1, source_target_pairs={{0,1},{2,3},{4,5},{6,7},{8,9},{10,11},{12,13},{14,15},{1,0},{3,2},... | collective-permute-start | bytes 36872 | tf_op jit(solution)/shard_map/ppermute | solution.py:358

commit v3 on v0

v3 whole, which is shorter than its diff:
```python
import functools

import jax
import jax.numpy as jnp
from jax import lax
from jax.experimental import pallas as pl
from jax.experimental.pallas import tpu as pltpu
from jax.sharding import PartitionSpec as P

ASTEPS = 3
OSTEPS = 2
COUPLE = 2

ADVECTION = 0.1
OCEAN_GAIN = 0.5
OCEAN_DIFFUSION = 0.15

ANY = pl.BlockSpec(memory_space=pl.ANY)
VMEM = pl.BlockSpec(memory_space=pltpu.VMEM)
SMEM = pl.BlockSpec(memory_space=pltpu.SMEM)
LANES = 128
QUARTERS = 4


def place(up, row, base, count):
    return jnp.where(up == 1, row - base, count - 1 - (row - base))


class Rows:
    def __init__(self, up, *pieces):
        self.up, self.pieces = up, pieces

    def at(self, row):
        for ref, base, count in self.pieces:
            if base <= row < base + count:
                return ref, place(self.up, row, base, count)
        raise IndexError(row)


def sea_piece(ref, row, c, t, lon):
    per = lon // QUARTERS // LANES
    line, part = c * QUARTERS + t // per, t % per
    return ref[row, line : line + 1, part * LANES : (part + 1) * LANES]


def atmos_rows(reals, coef, source, target, surface, rows, edge=None, valid=None):
    level = lax.broadcasted_iota(jnp.int32, (8, LANES), 0)
    lane = lax.broadcasted_iota(jnp.int32, (8, LANES), 1)
    for row in rows:
        src, here = source.at(row)
        src_s, south = source.at(row - 1)
        src_n, north = source.at(row + 1)
        dst, there = target.at(row)
        srf, sea = surface.at(row)
        members, lon = src.shape[1], src.shape[4]
        tiles = lon // LANES
        for m in range(members):
            diffusivity = reals[m]
            keep = 1.0 - 4.0 * diffusivity
            centres, easts, wests = {}, {}, {}
            for step in range(tiles + 2):
                ahead = step % tiles
                for c in (1, 0):
                    if (c, ahead) not in centres:
                        piece = src[c, m, here, :, ahead * LANES : (ahead + 1) * LANES]
                        centres[c, ahead] = piece
                        easts[c, ahead] = pltpu.roll(piece, LANES - 1, 1)
                        wests[c, ahead] = pltpu.roll(piece, 1, 1)
                if step < 2:
                    continue
                t = (step - 1) % tiles
                before, after = (t - 1) % tiles, (t + 1) % tiles
                span = slice(t * LANES, (t + 1) * LANES)
                wind = (0.5 * ADVECTION) * centres[1, t]
                for c in (1, 0):
                    eastern = jnp.where(lane == LANES - 1, easts[c, after], easts[c, t])
                    western = jnp.where(lane == 0, wests[c, before], wests[c, t])
                    beside = src_s[c, m, south, :, span] + src_n[c, m, north, :, span]
                    part = (
                        keep * centres[c, t]
                        + diffusivity * (beside + (eastern + western))
                        - wind * (eastern - western)
                    )
                    total = coef[c, m, 0] * part
                    for d in range(1, 8):
                        total += coef[c, m, d] * pltpu.roll(part, 8 - d, 0)
                    relax = jnp.where(level == 0, reals[members + c * members + m], 0.0)
                    total += relax * sea_piece(srf, sea, c, t, lon)
                    if edge is not None and row >= edge:
                        total = total * valid
                    dst[c, m, there, :, span] = total


def flux_rows(reals, state, surface, out, rows, ensemble):
    for row in rows:
        st, at = state.at(row)
        srf, sea = surface.at(row)
        ref, to = out.at(row)
        members, lon = st.shape[1], st.shape[4]
        per = lon // QUARTERS // LANES
        for c in range(2):
            for t in range(lon // LANES):
                s = sea_piece(srf, sea, c, t, lon)
                flux = jnp.zeros_like(s)
                for m in range(members):
                    flux += reals[members + c * members + m] * (st[c, m, at, 0:1, t * LANES : (t + 1) * LANES] - s)
                line, part = c * QUARTERS + t // per, t % per
                ref[to, line : line + 1, part * LANES : (part + 1) * LANES] = flux * (1.0 / ensemble)


def ocean_rows(sea, ocean, forcing, target, rows):
    for row in rows:
        src, here = ocean.at(row)
        src_s, south = ocean.at(row - 1)
        src_n, north = ocean.at(row + 1)
        fixed, cell = sea.at(row)
        frc, force = forcing.at(row)
        dst, to = target.at(row)
        centre = src[here]
        lines, lon = centre.shape
        line = lax.broadcasted_iota(jnp.int32, (lines, lon), 0)
        lane = lax.broadcasted_iota(jnp.int32, (lines, lon), 1)
        quarter = line % QUARTERS
        both = fixed[cell]
        turned = pltpu.roll(both, QUARTERS, 0)
        mask = jnp.where(line < QUARTERS, turned, both)
        rate = jnp.where(line < QUARTERS, OCEAN_DIFFUSION, turned)
        eastern, western = pltpu.roll(centre, lon - 1, 1), pltpu.roll(centre, 1, 1)
        after = jnp.where(quarter == QUARTERS - 1, pltpu.roll(eastern, QUARTERS - 1, 0), pltpu.roll(eastern, lines - 1, 0))
        before = jnp.where(quarter == 0, pltpu.roll(western, lines - QUARTERS + 1, 0), pltpu.roll(western, 1, 0))
        eastern = jnp.where(lane == lon - 1, after, eastern)
        western = jnp.where(lane == 0, before, western)
        laplace = (eastern + western) + (src_s[south] + src_n[north]) - 4.0 * centre
        dst[to] = centre + mask * (OCEAN_GAIN * frc[force] + rate * laplace)


def started(source, target, sem):
    copy = pltpu.make_async_copy(source, target, sem)
    copy.start()
    return copy


def sea_of(up, band, low, own, high, part):
    return Rows(up, (low.at[:, part], -band, band), (own.at[:, part], 0, band), (high.at[:, part], band, band))


def gather_columns(width, ints, ocean, viscosity, mask, out):
    for row in range(ocean.shape[0]):
        out[row, 0:2, :] = ocean[row]
        out[row, 2:3, :] = viscosity[row : row + 1, :]
        piece = mask[row : row + 1, pl.ds(pl.multiple_of(ints[1] * width, LANES), width)]
        out[row, 3:4, :] = piece.astype(jnp.float32)


def pack_rows(cfg, ints, own, other, out):
    side = ints[1]
    rows, _, lines, size = out.shape
    parts = own.shape[2] // size
    for row in range(rows):
        for field in range(4):
            for part in range(parts):
                line = (field % 2) * QUARTERS + part
                for ref, half in ((own, side), (other, 1 - side)):
                    out[row, field // 2, pl.ds(line + half * parts, 1), :] = ref[
                        row, field : field + 1, part * size : (part + 1) * size
                    ]


def inner_first(cfg, ints, reals, coef, a_low, a_in, a_out, sea_low, sea_own,
                done, carry1, carry2, flux, lev1, lev2, keep1, keep2, sems):
    band, H, ensemble = cfg
    up = ints[0]
    surface = Rows(up, (sea_low.at[:, 0], -band, band), (sea_own.at[:, 0], 0, band))
    inner(up, cfg, reals, coef, surface, a_low, a_in, a_out, done, carry1, carry2, flux, lev1, lev2, keep1, keep2, sems)


def inner(up, cfg, reals, coef, surface, a_low, a_in, a_out, done, carry1, carry2, flux, lev1, lev2, keep1, keep2, sems):
    band, H, ensemble = cfg
    step0 = Rows(up, (a_low, -H, H), (a_in, 0, H), (a_out, H, H))
    step1 = Rows(up, (lev1, -2, 5), (keep1, 3, 2))
    step2 = Rows(up, (lev2, -1, 3), (keep2, 2, 2))
    step3 = Rows(up, (done, 0, H))
    atmos_rows(reals, coef, step0, step1, surface, range(-2, 5))
    first = started(keep1, carry1, sems.at[0])
    atmos_rows(reals, coef, step1, step2, surface, range(-1, 4))
    second = started(keep2, carry2, sems.at[1])
    atmos_rows(reals, coef, step2, step3, surface, range(0, 3))
    flux_rows(reals, step3, surface, Rows(up, (flux, 0, H)), range(H), ensemble)
    first.wait()
    second.wait()


def inner_second(cfg, ints, reals, coef, a_low, a_in, a_out, sea_low, sea_own, sea_high, f_low, f_own,
                 done, carry1, carry2, flux, surf_out, surf, middle, lev1, lev2, keep1, keep2, sems):
    band, H, ensemble = cfg
    up = ints[0]
    start, fixed = (sea_of(up, band, sea_low, sea_own, sea_high, part) for part in range(2))
    forcing = Rows(up, (f_low, -band, band), (f_own, 0, band))
    half, surface = Rows(up, (middle, -3, 9)), Rows(up, (surf, -2, 7))
    ocean_rows(fixed, start, forcing, half, range(-3, 6))
    ocean_rows(fixed, half, forcing, surface, range(-2, 5))
    third = started(surf, surf_out, sems.at[2])
    inner(up, cfg, reals, coef, surface, a_low, a_in, a_out, done, carry1, carry2, flux, lev1, lev2, keep1, keep2, sems)
    third.wait()


def outer_first(cfg, ints, reals, coef, a_out, a_high, carry1, carry2, flux_in, sea_own, sea_high,
                done, next1, next2, flux, lev1, lev2, keep1, keep2, made1, made2, part, sems):
    band, H, ensemble = cfg
    up, valid = ints[0], reals[reals.shape[0] - 1]
    surface = Rows(up, (sea_own.at[:, 0], 0, band), (sea_high.at[:, 0], band, band))
    step0 = Rows(up, (a_out, 3, 3), (a_high, 6, 3))
    loads = [started(carry1, keep1, sems.at[0]), started(carry2, keep2, sems.at[1]), started(flux_in, part, sems.at[2])]
    step1 = Rows(up, (keep1, 3, 2), (lev1, 5, 1), (made1, 6, 2))
    step2 = Rows(up, (keep2, 2, 2), (lev2, 4, 1), (made2, 5, 2))
    step3 = Rows(up, (done, 3, 3))
    atmos_rows(reals, coef, step0, step1, surface, range(5, 8), band, valid)
    first = started(made1, next1, sems.at[3])
    for copy in loads:
        copy.wait()
    atmos_rows(reals, coef, step1, step2, surface, range(4, 7), band, valid)
    second = started(made2, next2, sems.at[4])
    atmos_rows(reals, coef, step2, step3, surface, range(3, 6), band, valid)
    join_flux(up, H, band, part, flux)
    flux_rows(reals, step3, surface, Rows(up, (flux, 0, band)), range(3, 6), ensemble)
    first.wait()
    second.wait()


def join_flux(up, H, band, flux_in, flux):
    source, target = Rows(up, (flux_in, 0, H)), Rows(up, (flux, 0, band))
    for row in range(H):
        (src, here), (dst, there) = source.at(row), target.at(row)
        dst[there] = src[here]


def outer_halo(cfg, ints, reals, coef, a_high, a_far, carry1, carry2, sea_high, done, lev1, lev2, keep1, keep2, sems):
    band, H, ensemble = cfg
    up, valid = ints[0], reals[reals.shape[0] - 1]
    surface = Rows(up, (sea_high.at[:, 0], band, band))
    step0 = Rows(up, (a_high, 6, 3), (a_far, 9, 3))
    loads = [started(carry1, keep1, sems.at[0]), started(carry2, keep2, sems.at[1])]
    step1 = Rows(up, (keep1, 6, 2), (lev1, 8, 3))
    step2 = Rows(up, (keep2, 5, 2), (lev2, 7, 3))
    step3 = Rows(up, (done, 6, 3))
    atmos_rows(reals, coef, step0, step1, surface, range(8, 11), band, valid)
    for copy in loads:
        copy.wait()
    atmos_rows(reals, coef, step1, step2, surface, range(7, 10), band, valid)
    atmos_rows(reals, coef, step2, step3, surface, range(6, 9), band, valid)


def outer_second(cfg, ints, reals, coef, b_out, b_high, b_carry1, b_carry2, b_in, flux_in, s_in,
                 sea_low, sea_own, sea_high, f_low, f_own, f_high,
                 result, flux, s_out, middle, lev1, lev2, done, keep1, keep2, part, s_kept, sems):
    band, H, ensemble = cfg
    up, valid = ints[0], reals[reals.shape[0] - 1]
    s_load = started(s_in, s_kept, sems.at[2])
    loads = [started(b_carry1, keep1, sems.at[3]), started(b_carry2, keep2, sems.at[4]), started(flux_in, part, sems.at[5])]
    first = pltpu.make_async_copy(b_in, result.at[:, :, pl.ds(jnp.where(up == 1, 0, H), H)], sems.at[0])
    first.start()
    start, fixed = (sea_of(up, band, sea_low, sea_own, sea_high, part) for part in range(2))
    forcing = Rows(up, (f_own, 0, band), (f_high, band, band))
    half = Rows(up, (middle, 4, 5))
    surface = Rows(up, (s_kept, -2, 7), (s_out, 5, 3))
    ocean_rows(fixed, start, forcing, half, range(4, 9))
    ocean_rows(fixed, half, forcing, surface, range(5, 8))
    step0 = Rows(up, (b_out, 3, 3), (b_high, 6, 3))
    step1 = Rows(up, (keep1, 3, 2), (lev1, 5, 3))
    step2 = Rows(up, (keep2, 2, 2), (lev2, 4, 3))
    step3 = Rows(up, (done, 3, 3))
    atmos_rows(reals, coef, step0, step1, surface, range(5, 8), band, valid)
    s_load.wait()
    for copy in loads:
        copy.wait()
    atmos_rows(reals, coef, step1, step2, surface, range(4, 7), band, valid)
    atmos_rows(reals, coef, step2, step3, surface, range(3, 6), band, valid)
    second = pltpu.make_async_copy(done, result.at[:, :, pl.ds(jnp.where(up == 1, H, 0), H)], sems.at[1])
    second.start()
    join_flux(up, H, band, part, flux)
    flux_rows(reals, step3, surface, Rows(up, (flux, 0, band)), range(3, 6), ensemble)
    first.wait()
    second.wait()


def ocean_last(cfg, ints, s_in, s_out, sea_low, sea_own, sea_high, f_low, f_own, f_high, out, middle, final, s_kept, sems):
    band, H, width = cfg
    up = ints[0]
    fixed = sea_of(up, band, sea_low, sea_own, sea_high, 1)
    started(s_in, s_kept, sems.at[0]).wait()
    surface = Rows(up, (s_kept, -2, 7), (s_out, 5, 3))
    forcing = Rows(up, (f_low, -1, 1), (f_own, 0, band), (f_high, band, 1))
    half = Rows(up, (middle, -1, band + 2))
    ocean_rows(fixed, surface, forcing, half, range(-1, band + 1))
    if width is None:
        ocean_rows(fixed, half, forcing, Rows(up, (out, 0, band)), range(band))
        return
    ocean_rows(fixed, half, forcing, Rows(up, (final, 0, band)), range(band))
    lon = final.shape[2]
    for row in range(band):
        for c in range(2):
            for part in range(width // lon):
                line = c * QUARTERS + ints[1] * (width // lon) + part
                out[row, c : c + 1, part * lon : (part + 1) * lon] = final[row, pl.ds(line, 1), :]


def call(kernel, cfg, outs, scratch, args, copies=0, flops=0):
    kinds = {"any": ANY, "vmem": VMEM, "smem": SMEM}
    return pl.pallas_call(
        functools.partial(kernel, cfg),
        name=kernel.__name__,
        out_shape=[jax.ShapeDtypeStruct(shape, jnp.float32) for _, shape in outs],
        in_specs=[kinds[kind] for kind, _ in args],
        out_specs=[kinds[kind] for kind, _ in outs],
        scratch_shapes=[pltpu.VMEM(shape, jnp.float32) for shape in scratch]
        + [pltpu.SemaphoreType.DMA((copies,))] * (copies > 0),
        compiler_params=pltpu.CompilerParams(vmem_limit_bytes=20 * 1024 * 1024),
        cost_estimate=pl.CostEstimate(flops=flops, bytes_accessed=4 * 1024 * 1024, transcendentals=0),
    )(*[value for _, value in args])


def lookup(parameter_index, parameter_table):
    onehot = (
        parameter_index[:, None] == jnp.arange(parameter_table.shape[0], dtype=jnp.int32)[None, :]
    ).astype(jnp.float32)
    picked = jnp.dot(
        onehot, parameter_table, precision=lax.Precision.HIGHEST, preferred_element_type=jnp.float32
    )
    return (0.6 * picked[:, 0], 2.0 * jnp.transpose(picked[:, 1:3]))


def mixing(level_mix, exchange):
    levels = level_mix.shape[0]
    ids = jnp.arange(levels)
    pick = (ids[None, None, :] == (ids[None, :, None] + ids[:, None, None]) % levels).astype(jnp.float32)
    whole = level_mix + jnp.eye(levels, dtype=jnp.float32)
    turned = jnp.sum(pick * whole[None], axis=2)
    scale = jnp.where(ids == 0, 1.0 - exchange[:, :, None], 1.0)
    coef = turned[None, None] * scale[:, :, None, :]
    return jnp.broadcast_to(coef[..., None], coef.shape + (LANES,))


def body(atmosphere, ocean_state, viscosity, sea_mask, parameter_index, parameter_table, level_mix):
    H = ASTEPS
    fields, members, levels, band, lon = atmosphere.shape
    width = ocean_state.shape[2]
    sides, bands = lax.axis_size("member"), lax.axis_size("lat")
    ensemble = members * sides
    position = lax.axis_index("lat")
    side = lax.axis_index("member")
    up = position % 2
    near = [(i, i + 1) for i in range(0, bands, 2)]
    near += [(b, a) for a, b in near]
    far = [(i, i + 1) for i in range(1, bands - 1, 2)]
    far += [(b, a) for a, b in far]
    other = [(0, 1), (1, 0)]

    def rows(n):
        return (fields, members, n, levels, lon)

    def band_shape(n):
        return (n, fields * QUARTERS, lon // QUARTERS)

    def vmem(*values):
        return [("vmem", value) for value in values]

    def anywhere(*values):
        return [("any", value) for value in values]

    def to_near(x):
        return lax.ppermute(x, "lat", near)

    def to_far(x):
        return lax.ppermute(x, "lat", far)

    def total(x):
        if sides == 2:
            return x + lax.ppermute(x, "member", other)
        return lax.psum(x, "member")

    def total_beside(x, work):
        if sides == 2:
            y, work = lax.optimization_barrier((lax.ppermute(x, "member", other), work))
            return x + y, work
        return lax.psum(x, "member"), work

    def full_rows(x):
        if sides == 2:
            y = lax.ppermute(x, "member", other)
            if whole_quarters:
                (packed,) = call(pack_rows, None, vmem((band, 2, fields * QUARTERS, lon // QUARTERS)), [], [("smem", ints)] + vmem(x, y))
                return packed
            low, high = jnp.where(side == 0, x, y), jnp.where(side == 0, y, x)
            whole = jnp.concatenate([low, high], axis=2)
        else:
            whole = lax.all_gather(x, "member", axis=2, tiled=True)
        return whole.reshape(band, 2, fields * QUARTERS, lon // QUARTERS)

    state = jnp.transpose(atmosphere, (0, 1, 3, 2, 4))
    ints = jnp.stack([up, side]).astype(jnp.int32)
    whole_quarters = width % (lon // QUARTERS) == 0
    turned_ocean = jnp.transpose(ocean_state, (1, 0, 2))
    if width % LANES == 0:
        (columns,) = call(
            gather_columns, width, vmem((band, 4, width)), [],
            [("smem", ints)] + vmem(turned_ocean, viscosity, sea_mask))
    else:
        mask = lax.dynamic_slice_in_dim(sea_mask, side * width, width, 1).astype(jnp.float32)
        columns = jnp.concatenate([turned_ocean, viscosity[:, None], mask[:, None]], axis=1)
    far_columns = to_far(columns)
    columns, start = lax.optimization_barrier((columns, up))
    a_out = lax.dynamic_slice_in_dim(state, start * H, H, 2)
    a_high = to_far(a_out)
    later, a_out = lax.optimization_barrier((start, a_out))
    a_in = lax.dynamic_slice_in_dim(state, (1 - later) * H, H, 2)
    a_low = to_near(a_in)
    sea_own = full_rows(columns)
    sea_low = to_near(sea_own)
    far_columns, a_low = lax.optimization_barrier((far_columns, a_low))
    sea_high = full_rows(far_columns)

    diffusivity, exchange = lookup(parameter_index, parameter_table)
    coef = mixing(level_mix, exchange)
    valid = jnp.where(up == 1, position < bands - 1, position > 0).astype(jnp.float32)
    reals = jnp.concatenate([diffusivity, exchange.reshape(-1), valid[None]])
    common = [("smem", ints), ("smem", reals), ("vmem", coef)]
    cfg = (band, H, ensemble)
    unit = members * fields * levels * lon * 30
    carries = anywhere(rows(2), rows(2))
    inner_outs = vmem(rows(H)) + carries + vmem(band_shape(H))
    kept = [rows(2), rows(2)]

    b_in, carry1, carry2, flux = call(
        inner_first, cfg, inner_outs, [rows(5), rows(3)] + kept,
        common + vmem(a_low, a_in, a_out, sea_low, sea_own), 2, flops=15 * unit)
    a_far = to_far(a_in)
    b_low = to_near(b_in)
    b_out, carry1, carry2, flux = call(
        outer_first, cfg, vmem(rows(H)) + carries + vmem(band_shape(band)), [rows(1), rows(1)] + kept * 2 + [band_shape(H)],
        common + vmem(a_out, a_high) + anywhere(carry1, carry2, flux) + vmem(sea_own, sea_high), 5, flops=9 * unit)
    (b_high,) = call(
        outer_halo, cfg, vmem(rows(H)), [rows(3), rows(3)] + kept,
        common + vmem(a_high, a_far) + anywhere(carry1, carry2) + vmem(sea_high), 2, flops=9 * unit)
    f_own, b_high = total_beside(flux, b_high)
    f_low, f_high = to_near(f_own), to_far(f_own)
    c_in, b_carry1, b_carry2, flux, s_in = call(
        inner_second, cfg, inner_outs + anywhere(band_shape(7)), [band_shape(7), band_shape(9), rows(5), rows(3)] + kept,
        common + vmem(b_low, b_in, b_out, sea_low, sea_own, sea_high, f_low, f_own), 3, flops=15 * unit)
    result, flux, s_out = call(
        outer_second, cfg, [("any", rows(band))] + vmem(band_shape(band), band_shape(3)),
        [band_shape(5), rows(3), rows(3), rows(3)] + kept + [band_shape(H), band_shape(7)],
        common + vmem(b_out, b_high) + anywhere(b_carry1, b_carry2, c_in, flux, s_in)
        + vmem(sea_low, sea_own, sea_high, f_low, f_own, f_high),
        copies=6, flops=9 * unit)
    g_own = total(flux)
    g_low = to_near(lax.dynamic_slice_in_dim(g_own, (1 - up) * (band - 1), 1, 0))
    g_high = to_far(lax.dynamic_slice_in_dim(g_own, up * (band - 1), 1, 0))
    (ocean,) = call(
        ocean_last, (band, H, width if whole_quarters else None),
        vmem((band, fields, width) if whole_quarters else band_shape(band)), [band_shape(band + 2), band_shape(band), band_shape(7)],
        [("smem", ints)] + anywhere(s_in) + vmem(s_out, sea_low, sea_own, sea_high, g_low, g_own, g_high), 1)
    if not whole_quarters:
        ocean = lax.dynamic_slice_in_dim(ocean.reshape(band, fields, lon), side * width, width, 2)
    return (jnp.transpose(result, (0, 1, 3, 2, 4)), jnp.transpose(ocean, (1, 0, 2)))


def solution(mesh):
    return jax.shard_map(
        body,
        mesh=mesh,
        in_specs=(
            P(None, "member", None, "lat", None),
            P(None, "lat", "member"),
            P("lat", "member"),
            P("lat", None),
            P("member"),
            P(),
            P(),
        ),
        out_specs=(P(None, "member", None, "lat", None), P(None, "lat", "member")),
        check_vma=False,
    )
```

time: 153 us -> 67 us (0.44)
  starting transfers between devices: 54.8 us -> 22.2 us
  Pallas kernels: 0 us -> 26.1 us
  matrix products: 20.7 us -> 0.18 us
  local copies, waits for them, and re-layouts: 21.9 us -> 2.87 us
  between operations: 14.9 us -> 1.12 us
  other arithmetic: 10.2 us -> 0.69 us
  blocking collectives: 9.4 us -> 0 us
  waiting for transfers between devices: 20.6 us -> 12.6 us
    ppermute x24 -> x14, starting transfers between devices: 54.8 us -> 22.2 us  [the longest x5 14.4 us: to_far(): return lax.ppermute(x, 'lat', far)]
    pallas_call x0 -> x9, Pallas kernels: none -> 26.1 us  [call(): pl.pallas_call(functools.partial(kernel, cfg), name=kernel.__name__, out_...]
    dot_general x6 -> x0, matrix products: 20.5 us -> none  [atmos_step(): jnp.einsum('kl,fmlrn->fmkrn', level_mix, advected, precision=lax.Precisio...]
    scatter x6 -> x0, local copies, waits for them, and re-layouts: 11.2 us -> none  [atmos_step(): return mixed_state.at[:, :, 0].set(bottom)]
    reduce_scatter x2 -> x0, waiting for transfers between devices: 10 us -> none  [body(): lax.psum_scatter(flux_terms, 'member', scatter_dimension=2, tiled=True)]
    all_gather x2 -> x0, blocking collectives: 9.4 us -> none  [body(): surface = lax.all_gather(ocean, 'member', axis=2, tiled=True)]
    slice x33 -> x0, local copies, waits for them, and re-layouts: 7.73 us -> none  [the longest x10 3.13 us: atmos_step(): eastern = jnp.roll(centre, -1, axis=4)]
    add x10 -> x3, other arithmetic: 5.84 us -> 0.03 us  [the longest x1 0.01 us: total_beside(): return (x + y, work)]
  transfers between devices with their start and end apart: 26 -> 14, of which waited for: 8 -> 5; matrix products, arithmetic and copies ran while one was open for 30% -> 2% of each run, Pallas kernels for 0% -> 30%
where the time goes in v3:
time: 67 us; the launch traced here: 65.9 us
  Pallas kernels  26.1 us (39%)
  starting transfers between devices  22.2 us (33%)
  waiting for transfers between devices  12.6 us (19%)
  local copies, waits for them, and re-layouts  2.87 us (4%)
  between operations  1.12 us (2%)
  other arithmetic  0.69 us (1%)
    pallas_call x9, Pallas kernels, call(): pl.pallas_call(functools.partial(kernel, cfg), name=kernel.__name__, out_...  26.1 us
    ppermute x5, starting transfers between devices, to_far(): return lax.ppermute(x, 'lat', far)  14.4 us
    ppermute x2, waiting for transfers between devices, full_rows(): y = lax.ppermute(x, 'member', other)  5.6 us
    ppermute x1, waiting for transfers between devices, total(): return x + lax.ppermute(x, 'member', other)  3.2 us
    ppermute x2, starting transfers between devices, full_rows(): y = lax.ppermute(x, 'member', other)  3.06 us
    ppermute x5, waiting for transfers between devices, to_far(): return lax.ppermute(x, 'lat', far)  2.84 us
    unnamed x14, local copies, waits for them, and re-layouts  2.41 us
    ppermute x5, starting transfers between devices, to_near(): return lax.ppermute(x, 'lat', near)  1.68 us
  transfers between devices with their start and end apart: 14, of which 5 were waited for; matrix products, arithmetic and copies ran while one was open for 2% of the time, Pallas kernels for 30%

profile of v3, /device:TPU:8, one launch (start us, length us, event | category | flops | bytes accessed | tf_op | source)
XLA Modules:
  0.0 65.9 jit_solution(8377915608715855992)
XLA Ops:
  0.7 0.9 %copy-done.1 = s32[6,1536]{1,0:T(8,128)S(1)} copy-done((s32[6,1536]{1,0:T(8,128)S(1)}, s32[6,1536]{1,0:T(8,128)}, u32[]{:S(2)}) %copy-start.1) | copy-done | bytes 36888
  1.6 0.8 %copy-done.2 = f32[2,6,768]{2,0,1:T(2,128)S(1)} copy-done((f32[2,6,768]{2,0,1:T(2,128)S(1)}, f32[2,6,768]{2,0,1:T(2,128)}, u32[]{:S(2)}) %copy-start.2) | copy-done | bytes 36888
  2.4 0.7 %copy-done.3 = f32[6,768]{1,0:T(8,128)S(1)} copy-done((f32[6,768]{1,0:T(8,128)S(1)}, f32[6,768]{1,0:T(8,128)}, u32[]{:S(2)}) %copy-start.3) | copy-done | bytes 18456
  3.7 2.8 %collective-permute-start.1 = (f32[6,4,768]{2,1,0:T(4,128)S(1)}, f32[6,4,768]{2,1,0:T(4,128)S(1)}, u32[]{:S(2)}, u32[]{:S(2)}) collective-permute-start(f32[6,4,768]{2,1,0:T(4,128)S(1)} %gather_columns.1.own), channel_id=1, source_target_pairs={{1,2},{3,4},{5,6},{7,8},{9,10},{11,12},{13,14},{2,1},{4,3},{6,5},{... | collective-permute-start | bytes 221192 | tf_op jit(solution)/shard_map/ppermute | solution.py:374
  6.6 3.7 %collective-permute-start = (f32[2,2,3,8,1536]{4,3,2,1,0:T(8,128)S(1)}, f32[2,2,3,8,1536]{4,3,2,1,0:T(8,128)S(1)}, u32[]{:S(2)}, u32[]{:S(2)}) collective-permute-start(f32[2,2,3,8,1536]{4,3,2,1,0:T(8,128)S(1)} %dynamic-slice_bitcast_fusion.1.a_out), channel_id=1, source_target_pairs={{1,2},{3,4},{5,6},{7,8},{9,10},{11,12},{13,14},{2,1},{4,3},{6,5},{... | collective-permute-start | bytes 1769480 | tf_op jit(solution)/shard_map/ppermute | solution.py:374
  10.4 2.8 %collective-permute-start.7 = (f32[2,2,3,8,1536]{4,3,2,1,0:T(8,128)S(1)}, f32[2,2,3,8,1536]{4,3,2,1,0:T(8,128)}, u32[]{:S(2)}, u32[]{:S(2)}) collective-permute-start(f32[2,2,3,8,1536]{4,3,2,1,0:T(8,128)S(1)} %dynamic-slice_bitcast_fusion.a_in), channel_id=1, source_target_pairs={{1,2},{3,4},{5,6},{7,8},{9,10},{11,12},{13,14},{2,1},{4,3},{6,5},{... | collective-permute-start | bytes 1769480 | tf_op jit(solution)/shard_map/ppermute | solution.py:374
  13.2 1.6 %collective-permute-start.3 = (f32[6,4,768]{2,1,0:T(4,128)S(1)}, f32[6,4,768]{2,1,0:T(4,128)S(1)}, u32[]{:S(2)}, u32[]{:S(2)}) collective-permute-start(f32[6,4,768]{2,1,0:T(4,128)S(1)} %gather_columns.1.own), channel_id=1, source_target_pairs={{0,16},{16,0},{1,17},{17,1},{2,18},{18,2},{3,19},{19,3},{4,20},{20... | collective-permute-start | bytes 221192 | tf_op jit(solution)/shard_map/ppermute | solution.py:389
  15.4 2.6 %collective-permute-done.3.other = f32[6,4,768]{2,1,0:T(4,128)S(1)} collective-permute-done((f32[6,4,768]{2,1,0:T(4,128)S(1)}, f32[6,4,768]{2,1,0:T(4,128)S(1)}, u32[]{:S(2)}, u32[]{:S(2)}) %collective-permute-start.3) | collective-permute-done | bytes 73760 | tf_op jit(solution)/shard_map/ppermute | solution.py:389
  19.1 1.0 %collective-permute-done.4.sea_low = f32[6,2,8,384]{3,2,1,0:T(8,128)S(1)} collective-permute-done((f32[6,2,8,384]{3,2,1,0:T(8,128)S(1)}, f32[6,2,8,384]{3,2,1,0:T(8,128)S(1)}, u32[]{:S(2)}, u32[]{:S(2)}) %collective-permute-start.4) | collective-permute-done | bytes 147488 | tf_op jit(solution)/shard_map/ppermute | solution.py:371
  20.2 5.4 %inner_first.1 = (f32[2,2,3,8,1536]{4,3,2,1,0:T(8,128)S(1)}, f32[2,2,2,8,1536]{4,3,2,1,0:T(8,128)S(1)}, f32[2,2,2,8,1536]{4,3,2,1,0:T(8,128)S(1)}, f32[3,8,384]{2,1,0:T(8,128)S(1)}) custom-call(s32[2]{0:T(128)S(1)} %pad_add_fusion.ints, f32[7]{0:T(128)S(1)} %pad_maximum_fusion.reals, f32[2,2,8,8,128]{4,3,2,1,0:T(8,128)S(1)} %broadcast_in_dim.42.coef, ...), custom_call_target="tpu_custom_call" | custom-call | flops 22118400 | bytes 4194304 | tf_op jit(solution)/shard_map/inner_first/pallas_call | solution.py:309
  25.7 1.5 %collective-permute-start.5 = (f32[6,4,768]{2,1,0:T(4,128)S(1)}, f32[6,4,768]{2,1,0:T(4,128)S(1)}, u32[]{:S(2)}, u32[]{:S(2)}) collective-permute-start(f32[6,4,768]{2,1,0:T(4,128)S(1)} %collective-permute-done.1.own), channel_id=1, source_target_pairs={{0,16},{16,0},{1,17},{17,1},{2,18},{18,2},{3,19},{19,3},{4,20},{20... | collective-permute-start | bytes 221192 | tf_op jit(solution)/shard_map/ppermute | solution.py:389
  27.2 3.0 %collective-permute-done.5.other = f32[6,4,768]{2,1,0:T(4,128)S(1)} collective-permute-done((f32[6,4,768]{2,1,0:T(4,128)S(1)}, f32[6,4,768]{2,1,0:T(4,128)S(1)}, u32[]{:S(2)}, u32[]{:S(2)}) %collective-permute-start.5) | collective-permute-done | bytes 73760 | tf_op jit(solution)/shard_map/ppermute | solution.py:389
  30.9 3.9 %outer_first.1 = (f32[2,2,3,8,1536]{4,3,2,1,0:T(8,128)S(1)}, f32[2,2,2,8,1536]{4,3,2,1,0:T(8,128)S(1)}, f32[2,2,2,8,1536]{4,3,2,1,0:T(8,128)S(1)}, f32[6,8,384]{2,1,0:T(8,128)S(1)}) custom-call(s32[2]{0:T(128)S(1)} %pad_add_fusion.ints, f32[7]{0:T(128)S(1)} %pad_maximum_fusion.reals, f32[2,2,8,8,128]{4,3,2,1,0:T(8,128)S(1)} %broadcast_in_dim.42.coef, ...), custom_call_target="tpu_custom_call" | custom-call | flops 13271040 | bytes 4194304 | tf_op jit(solution)/shard_map/outer_first/pallas_call | solution.py:309
  34.8 1.6 %collective-permute-start.6 = (f32[6,8,384]{2,1,0:T(8,128)S(1)}, f32[6,8,384]{2,1,0:T(8,128)S(1)}, u32[]{:S(2)}, u32[]{:S(2)}) collective-permute-start(f32[6,8,384]{2,1,0:T(8,128)S(1)} %get-tuple-element.36), channel_id=1, source_target_pairs={{0,16},{16,0},{1,17},{17,1},{2,18},{18,2},{3,19},{19,3},{4,20},{20... | collective-permute-start | bytes 221192 | tf_op jit(solution)/shard_map/ppermute | solution.py:383
  36.3 3.8 %outer_halo.1.b_high = f32[2,2,3,8,1536]{4,3,2,1,0:T(8,128)S(1)} custom-call(s32[2]{0:T(128)S(1)} %pad_add_fusion.ints, f32[7]{0:T(128)S(1)} %pad_maximum_fusion.reals, f32[2,2,8,8,128]{4,3,2,1,0:T(8,128)S(1)} %broadcast_in_dim.42.coef, f32[2,2,3,8,1536]{4,3,2,1,0:T(8,128)S(1)} %collective-permute-done.a_high, ...), custom_call_target="tpu_custom_call" | custom-call | flops 13271040 | bytes 4194304 | tf_op jit(solution)/shard_map/outer_halo/pallas_call | solution.py:309
  40.2 1.3 %collective-permute-start.9 = (f32[6,8,384]{2,1,0:T(8,128)S(1)}, f32[6,8,384]{2,1,0:T(8,128)S(1)}, u32[]{:S(2)}, u32[]{:S(2)}) collective-permute-start(f32[6,8,384]{2,1,0:T(8,128)S(1)} %add.62.f_own), channel_id=1, source_target_pairs={{0,1},{2,3},{4,5},{6,7},{8,9},{10,11},{12,13},{14,15},{1,0},{3,2},... | collective-permute-start | bytes 221192 | tf_op jit(solution)/shard_map/ppermute | solution.py:371
  41.4 2.1 %collective-permute-start.10 = (f32[6,8,384]{2,1,0:T(8,128)S(1)}, f32[6,8,384]{2,1,0:T(8,128)S(1)}, u32[]{:S(2)}, u32[]{:S(2)}) collective-permute-start(f32[6,8,384]{2,1,0:T(8,128)S(1)} %add.62.f_own), channel_id=1, source_target_pairs={{1,2},{3,4},{5,6},{7,8},{9,10},{11,12},{13,14},{2,1},{4,3},{6,5},{... | collective-permute-start | bytes 221192 | tf_op jit(solution)/shard_map/ppermute | solution.py:374
  43.6 5.3 %inner_second.1 = (f32[2,2,3,8,1536]{4,3,2,1,0:T(8,128)S(1)}, f32[2,2,2,8,1536]{4,3,2,1,0:T(8,128)S(1)}, f32[2,2,2,8,1536]{4,3,2,1,0:T(8,128)S(1)}, f32[3,8,384]{2,1,0:T(8,128)S(1)}, f32[7,8,384]{2,1,0:T(8,128)S(1)}) custom-call(s32[2]{0:T(128)S(1)} %pad_add_fusion.ints, f32[7]{0:T(128)S(1)} %pad_maximum_fusion.reals, ...), custom_call_target="tpu_custom_call" | custom-call | flops 22118400 | bytes 4194304 | tf_op jit(solution)/shard_map/inner_second/pallas_call | solution.py:309
  48.9 4.5 %outer_second.1 = (f32[2,2,6,8,1536]{4,3,2,1,0:T(8,128)}, f32[6,8,384]{2,1,0:T(8,128)S(1)}, f32[3,8,384]{2,1,0:T(8,128)S(1)}) custom-call(s32[2]{0:T(128)S(1)} %pad_add_fusion.ints, f32[7]{0:T(128)S(1)} %pad_maximum_fusion.reals, f32[2,2,8,8,128]{4,3,2,1,0:T(8,128)S(1)} %broadcast_in_dim.42.coef, f32[2,2,3,8,1536]{4,3,2,1,0:T(8,128)S(1)} %get-tuple-element.35.a_out.b_out, ...), custom_call_target="tpu_custom_call" | custom-call | flops 13271040 | bytes 4194304 | tf_op jit(solution)/shard_map/outer_second/pallas_call | solution.py:309
  53.4 1.6 %collective-permute-start.11 = (f32[6,8,384]{2,1,0:T(8,128)S(1)}, f32[6,8,384]{2,1,0:T(8,128)S(1)}, u32[]{:S(2)}, u32[]{:S(2)}) collective-permute-start(f32[6,8,384]{2,1,0:T(8,128)S(1)} %get-tuple-element.49), channel_id=1, source_target_pairs={{0,16},{16,0},{1,17},{17,1},{2,18},{18,2},{3,19},{19,3},{4,20},{20... | collective-permute-start | bytes 221192 | tf_op jit(solution)/shard_map/ppermute | solution.py:378
  54.9 3.2 %collective-permute-done.11 = f32[6,8,384]{2,1,0:T(8,128)S(1)} collective-permute-done((f32[6,8,384]{2,1,0:T(8,128)S(1)}, f32[6,8,384]{2,1,0:T(8,128)S(1)}, u32[]{:S(2)}, u32[]{:S(2)}) %collective-permute-start.11) | collective-permute-done | bytes 73760 | tf_op jit(solution)/shard_map/ppermute | solution.py:378
  58.2 3.1 %collective-permute-start.13 = (f32[1,8,384]{2,1,0:T(8,128)S(1)}, f32[1,8,384]{2,1,0:T(8,128)S(1)}, u32[]{:S(2)}, u32[]{:S(2)}) collective-permute-start(f32[1,8,384]{2,1,0:T(8,128)S(1)} %get-tuple-element.50), channel_id=1, source_target_pairs={{1,2},{3,4},{5,6},{7,8},{9,10},{11,12},{13,14},{2,1},{4,3},{6,5},{... | collective-permute-start | bytes 36872 | tf_op jit(solution)/shard_map/ppermute | solution.py:374
  61.3 2.8 %collective-permute-done.13.f_high = f32[1,8,384]{2,1,0:T(8,128)S(1)} collective-permute-done((f32[1,8,384]{2,1,0:T(8,128)S(1)}, f32[1,8,384]{2,1,0:T(8,128)S(1)}, u32[]{:S(2)}, u32[]{:S(2)}) %collective-permute-start.13) | collective-permute-done | bytes 12320 | tf_op jit(solution)/shard_map/ppermute | solution.py:374
  64.1 1.6 %ocean_last.1 = f32[6,2,768]{2,1,0:T(2,128)} custom-call(s32[2]{0:T(128)S(1)} %pad_add_fusion.ints, f32[7,8,384]{2,1,0:T(8,128)S(1)} %get-tuple-element.46.s_in, f32[3,8,384]{2,1,0:T(8,128)S(1)} %get-tuple-element.48.s_out, f32[6,2,8,384]{3,2,1,0:T(8,128)S(1)} %collective-permute-done.4.sea_low, f32[6,2,8,384]{3,2,1,0:T(8,128)S(1)} %pack_rows.2.sea_own, ...), custom_call_target="tpu_custom_call" | custom-call | bytes 4194304 | tf_op jit(solution)/shard_map/ocean_last/pallas_call | solution.py:309
  (48 shorter events, 3.6 us)
Async XLA Ops:
  0.6 5.8 %copy-start = (f32[2,2,8,6,1536]{4,2,3,1,0:T(8,128)S(1)}, f32[2,2,8,6,1536]{4,2,3,1,0:T(8,128)}, u32[]{:S(2)}) copy-start(f32[2,2,8,6,1536]{4,2,3,1,0:T(8,128)} %param.7) | copy-start | bytes 3538948
  0.7 0.9 %copy-start.1 = (s32[6,1536]{1,0:T(8,128)S(1)}, s32[6,1536]{1,0:T(8,128)}, u32[]{:S(2)}) copy-start(s32[6,1536]{1,0:T(8,128)} %mask.1) | copy-start | bytes 110596
  1.6 0.8 %copy-start.2 = (f32[2,6,768]{2,0,1:T(2,128)S(1)}, f32[2,6,768]{2,0,1:T(2,128)}, u32[]{:S(2)}) copy-start(f32[2,6,768]{2,0,1:T(2,128)} %param.8) | copy-start | bytes 110596
  2.4 0.7 %copy-start.3 = (f32[6,768]{1,0:T(8,128)S(1)}, f32[6,768]{1,0:T(8,128)}, u32[]{:S(2)}) copy-start(f32[6,768]{1,0:T(8,128)} %viscosity.1) | copy-start | bytes 55300
  3.7 15.4 %collective-permute-start.1 = (f32[6,4,768]{2,1,0:T(4,128)S(1)}, f32[6,4,768]{2,1,0:T(4,128)S(1)}, u32[]{:S(2)}, u32[]{:S(2)}) collective-permute-start(f32[6,4,768]{2,1,0:T(4,128)S(1)} %gather_columns.1.own), channel_id=1, source_target_pairs={{1,2},{3,4},{5,6},{7,8},{9,10},{11,12},{13,14},{2,1},{4,3},{6,5},{... | collective-permute-start | bytes 221192 | tf_op jit(solution)/shard_map/ppermute | solution.py:374
  6.5 8.3 %copy-start.5 = (f32[32,3]{0,1:T(4,128)S(1)}, f32[32,3]{0,1:T(4,128)}, u32[]{:S(2)}) copy-start(f32[32,3]{0,1:T(4,128)} %param.12) | copy-start | bytes 1156
  6.5 8.3 %copy-start.6 = (s32[2]{0:T(128)S(1)}, s32[2]{0:T(128)}, u32[]{:S(2)}) copy-start(s32[2]{0:T(128)} %param.11) | copy-start | bytes 28
  6.5 8.6 %copy-start.4 = (f32[8,8]{1,0:T(8,128)S(1)}, f32[8,8]{1,0:T(8,128)}, u32[]{:S(2)}) copy-start(f32[8,8]{1,0:T(8,128)} %param.13) | copy-start | bytes 772
  6.6 24.3 %collective-permute-start = (f32[2,2,3,8,1536]{4,3,2,1,0:T(8,128)S(1)}, f32[2,2,3,8,1536]{4,3,2,1,0:T(8,128)S(1)}, u32[]{:S(2)}, u32[]{:S(2)}) collective-permute-start(f32[2,2,3,8,1536]{4,3,2,1,0:T(8,128)S(1)} %dynamic-slice_bitcast_fusion.1.a_out), channel_id=1, source_target_pairs={{1,2},{3,4},{5,6},{7,8},{9,10},{11,12},{13,14},{2,1},{4,3},{6,5},{... | collective-permute-start | bytes 1769480 | tf_op jit(solution)/shard_map/ppermute | solution.py:374
  10.3 8.8 %collective-permute-start.2 = (f32[2,2,3,8,1536]{4,3,2,1,0:T(8,128)S(1)}, f32[2,2,3,8,1536]{4,3,2,1,0:T(8,128)}, u32[]{:S(2)}, u32[]{:S(2)}) collective-permute-start(f32[2,2,3,8,1536]{4,3,2,1,0:T(8,128)S(1)} %dynamic-slice_bitcast_fusion.a_in), channel_id=1, source_target_pairs={{0,1},{2,3},{4,5},{6,7},{8,9},{10,11},{12,13},{14,15},{1,0},{3,2},... | collective-permute-start | bytes 1769480 | tf_op jit(solution)/shard_map/ppermute | solution.py:371
  10.4 25.9 %collective-permute-start.7 = (f32[2,2,3,8,1536]{4,3,2,1,0:T(8,128)S(1)}, f32[2,2,3,8,1536]{4,3,2,1,0:T(8,128)}, u32[]{:S(2)}, u32[]{:S(2)}) collective-permute-start(f32[2,2,3,8,1536]{4,3,2,1,0:T(8,128)S(1)} %dynamic-slice_bitcast_fusion.a_in), channel_id=1, source_target_pairs={{1,2},{3,4},{5,6},{7,8},{9,10},{11,12},{13,14},{2,1},{4,3},{6,5},{... | collective-permute-start | bytes 1769480 | tf_op jit(solution)/shard_map/ppermute | solution.py:374
  13.2 4.8 %collective-permute-start.3 = (f32[6,4,768]{2,1,0:T(4,128)S(1)}, f32[6,4,768]{2,1,0:T(4,128)S(1)}, u32[]{:S(2)}, u32[]{:S(2)}) collective-permute-start(f32[6,4,768]{2,1,0:T(4,128)S(1)} %gather_columns.1.own), channel_id=1, source_target_pairs={{0,16},{16,0},{1,17},{17,1},{2,18},{18,2},{3,19},{19,3},{4,20},{20... | collective-permute-start | bytes 221192 | tf_op jit(solution)/shard_map/ppermute | solution.py:389
  18.6 1.4 %collective-permute-start.4 = (f32[6,2,8,384]{3,2,1,0:T(8,128)S(1)}, f32[6,2,8,384]{3,2,1,0:T(8,128)S(1)}, u32[]{:S(2)}, u32[]{:S(2)}) collective-permute-start(f32[6,2,8,384]{3,2,1,0:T(8,128)S(1)} %pack_rows.2.sea_own), channel_id=1, source_target_pairs={{0,1},{2,3},{4,5},{6,7},{8,9},{10,11},{12,13},{14,15},{1,0},{3,2},... | collective-permute-start | bytes 442376 | tf_op jit(solution)/shard_map/ppermute | solution.py:371
  25.5 18.0 %collective-permute-start.8 = (f32[2,2,3,8,1536]{4,3,2,1,0:T(8,128)S(1)}, f32[2,2,3,8,1536]{4,3,2,1,0:T(8,128)S(1)}, u32[]{:S(2)}, u32[]{:S(2)}) collective-permute-start(f32[2,2,3,8,1536]{4,3,2,1,0:T(8,128)S(1)} %get-tuple-element.40.a_in), channel_id=1, source_target_pairs={{0,1},{2,3},{4,5},{6,7},{8,9},{10,11},{12,13},{14,15},{1,0},{3,2},... | collective-permute-start | bytes 1769480 | tf_op jit(solution)/shard_map/ppermute | solution.py:371
  25.7 4.5 %collective-permute-start.5 = (f32[6,4,768]{2,1,0:T(4,128)S(1)}, f32[6,4,768]{2,1,0:T(4,128)S(1)}, u32[]{:S(2)}, u32[]{:S(2)}) collective-permute-start(f32[6,4,768]{2,1,0:T(4,128)S(1)} %collective-permute-done.1.own), channel_id=1, source_target_pairs={{0,16},{16,0},{1,17},{17,1},{2,18},{18,2},{3,19},{19,3},{4,20},{20... | collective-permute-start | bytes 221192 | tf_op jit(solution)/shard_map/ppermute | solution.py:389
  34.8 5.4 %collective-permute-start.6 = (f32[6,8,384]{2,1,0:T(8,128)S(1)}, f32[6,8,384]{2,1,0:T(8,128)S(1)}, u32[]{:S(2)}, u32[]{:S(2)}) collective-permute-start(f32[6,8,384]{2,1,0:T(8,128)S(1)} %get-tuple-element.36), channel_id=1, source_target_pairs={{0,16},{16,0},{1,17},{17,1},{2,18},{18,2},{3,19},{19,3},{4,20},{20... | collective-permute-start | bytes 221192 | tf_op jit(solution)/shard_map/ppermute | solution.py:383
  40.2 3.4 %collective-permute-start.9 = (f32[6,8,384]{2,1,0:T(8,128)S(1)}, f32[6,8,384]{2,1,0:T(8,128)S(1)}, u32[]{:S(2)}, u32[]{:S(2)}) collective-permute-start(f32[6,8,384]{2,1,0:T(8,128)S(1)} %add.62.f_own), channel_id=1, source_target_pairs={{0,1},{2,3},{4,5},{6,7},{8,9},{10,11},{12,13},{14,15},{1,0},{3,2},... | collective-permute-start | bytes 221192 | tf_op jit(solution)/shard_map/ppermute | solution.py:371
  41.4 7.4 %collective-permute-start.10 = (f32[6,8,384]{2,1,0:T(8,128)S(1)}, f32[6,8,384]{2,1,0:T(8,128)S(1)}, u32[]{:S(2)}, u32[]{:S(2)}) collective-permute-start(f32[6,8,384]{2,1,0:T(8,128)S(1)} %add.62.f_own), channel_id=1, source_target_pairs={{1,2},{3,4},{5,6},{7,8},{9,10},{11,12},{13,14},{2,1},{4,3},{6,5},{... | collective-permute-start | bytes 221192 | tf_op jit(solution)/shard_map/ppermute | solution.py:374
  53.4 4.8 %collective-permute-start.11 = (f32[6,8,384]{2,1,0:T(8,128)S(1)}, f32[6,8,384]{2,1,0:T(8,128)S(1)}, u32[]{:S(2)}, u32[]{:S(2)}) collective-permute-start(f32[6,8,384]{2,1,0:T(8,128)S(1)} %get-tuple-element.49), channel_id=1, source_target_pairs={{0,16},{16,0},{1,17},{17,1},{2,18},{18,2},{3,19},{19,3},{4,20},{20... | collective-permute-start | bytes 221192 | tf_op jit(solution)/shard_map/ppermute | solution.py:378
  58.1 3.2 %collective-permute-start.12 = (f32[1,8,384]{2,1,0:T(8,128)S(1)}, f32[1,8,384]{2,1,0:T(8,128)S(1)}, u32[]{:S(2)}, u32[]{:S(2)}) collective-permute-start(f32[1,8,384]{2,1,0:T(8,128)S(1)} %get-tuple-element.51), channel_id=1, source_target_pairs={{0,1},{2,3},{4,5},{6,7},{8,9},{10,11},{12,13},{14,15},{1,0},{3,2},... | collective-permute-start | bytes 36872 | tf_op jit(solution)/shard_map/ppermute | solution.py:371
  58.2 5.9 %collective-permute-start.13 = (f32[1,8,384]{2,1,0:T(8,128)S(1)}, f32[1,8,384]{2,1,0:T(8,128)S(1)}, u32[]{:S(2)}, u32[]{:S(2)}) collective-permute-start(f32[1,8,384]{2,1,0:T(8,128)S(1)} %get-tuple-element.50), channel_id=1, source_target_pairs={{1,2},{3,4},{5,6},{7,8},{9,10},{11,12},{13,14},{2,1},{4,3},{6,5},{... | collective-permute-start | bytes 36872 | tf_op jit(solution)/shard_map/ppermute | solution.py:374
